TPU v7x, 32 devices: a whole 2x2x4 slice. The times are simulated.
32 devices in a mesh: ctx: 4 (over z), ch: 8 (over y, x, core).
Axes of the slice: x: 2, y: 2, z: 4, core: 2. Of those that a mesh axis runs over, the one named last changes fastest.
Arguments:
- stream: bfloat16 [512, 8192], P('ctx', 'ch'), may hold values from -6 to 6
- in_weight: bfloat16 [8192, 3, 8192], P(None, None, 'ch'), may hold values from -0.0625 to 0.0625
- pole_rate: float32 [8192, 16], P('ch'), may hold values from 0.0009765625 to 0.05
- residue: float32 [8192, 16], P('ch'), may hold values from -1.5 to 1.5
- skip_gain: float32 [8192], P('ch'), may hold values from -4 to 4
- doc_lengths: int32 [8], replicated, may hold values from 1 to 256, 512 in all
Outputs:
- mixed: bfloat16 [512, 8192], P('ctx', 'ch')
Inputs may be any that keep to these rules, and one draw needn't show every extreme that they name: `doc_lengths`: the 8 documents lie end to end and cover the row: the lengths sum to 512, and the longest has exactly 512 // 2 tokens.
All inputs are finite; a program needn't handle non-finite values.
Results may differ from a plain program's by a relative error of at most 0.003.
Values may be sent and summed in bfloat16 or wider, within the bound.
No kernel may reach another device: no remote copies, remote signals or barrier semaphores. Data moves between devices by JAX's collectives and lax.ppermute only.
A program may use at most 192 MiB of HBM per device.

v0:
```python
import functools

import jax
import jax.numpy as jnp
from jax import lax
from jax.experimental import pallas as pl
from jax.experimental.pallas import tpu as pltpu
from jax.sharding import PartitionSpec as P

SUB = 8
LANE = 128
IN_VMEM = pl.BlockSpec(memory_space=pltpu.VMEM)
IN_SMEM = pl.BlockSpec(memory_space=pltpu.SMEM)
IN_HBM = pl.BlockSpec(memory_space=pl.ANY)


def shifted(block, axis, distance):
    devices = range(lax.axis_size(axis))
    route = [(i - distance, i) for i in devices if i - distance in devices]
    return lax.ppermute(block, axis, route)


def combine(earlier, later):
    return (earlier[0] * later[0], later[0] * earlier[1] + later[1])


def split_proj(product, squares, width, local):
    rowscale = lax.rsqrt(squares / width + 1e-06)
    proj = product * rowscale[:, None]
    outer = proj[:, :local]
    driven = proj[:, local : 2 * local] * proj[:, 2 * local :]
    return (outer, driven)


def local_scan(driven, keep, lam):
    modes, local = lam.shape
    decay = keep[:, None, None] * lam[None, :, :]
    drive = jnp.broadcast_to(driven[:, None, :], (driven.shape[0], modes, local))
    return lax.associative_scan(combine, (decay, drive), axis=0)


def general(stream, in_weight, pole_rate, residue, skip_gain, doc_lengths):
    rows = stream.shape[0]
    width = in_weight.shape[0]
    local = in_weight.shape[2]
    modes = pole_rate.shape[1]
    weights = in_weight.reshape(width, 3 * local)
    lam = jnp.exp(-pole_rate).T
    mix = (residue * jnp.sqrt(-jnp.expm1(-2.0 * pole_rate))).T
    starts = jnp.cumsum(doc_lengths) - doc_lengths
    position = lax.axis_index("ctx") * rows + jnp.arange(rows, dtype=jnp.int32)
    is_start = jnp.any(position[:, None] == starts[None, :], axis=1)
    keep = jnp.where(is_start, 0.0, 1.0).astype(jnp.float32)
    whole = lax.all_gather(stream, "ch", axis=1, tiled=True)
    floats = whole.astype(jnp.float32)
    squares = jnp.sum(floats * floats, axis=1)
    product = jnp.dot(whole, weights, preferred_element_type=jnp.float32)
    outer, driven = split_proj(product, squares, width, local)
    decay_cum, local_state = local_scan(driven, keep, lam)
    block_decay = decay_cum[-1]
    block_state = local_state[-1]
    zeros_state = jnp.zeros((modes, local), jnp.float32)

    def forward(step, incoming):
        outgoing = block_decay * incoming + block_state
        return shifted(outgoing, "ctx", 1)

    incoming = lax.fori_loop(0, lax.axis_size("ctx") - 1, forward, zeros_state)
    state = local_state + decay_cum * incoming[None, :, :]
    filtered = jnp.einsum("tnc,nc->tc", state, mix)
    return (outer * (filtered + skip_gain[None, :] * driven)).astype(jnp.bfloat16)


def chunk_rows(mask, depth):
    return pl.ds(pl.multiple_of((lax.axis_index("ch") ^ mask) * depth, depth), depth)


def add_squares(sq, blocks):
    total = sq
    for ref in blocks:
        for g in range(ref.shape[1] // LANE):
            v = ref[:, g * LANE : (g + 1) * LANE].astype(jnp.float32)
            total = total + v * v
    return total


def run_copies(copies, ahead):
    for c in copies[:ahead]:
        c.start()

    def wait(i):
        copies[i].wait()
        if i + ahead < len(copies):
            copies[i + ahead].start()

    return wait


def by_groups(value, store):
    for g in range(SUB):
        store(g, value[:, g * LANE : (g + 1) * LANE])


def first_kernel(o, s, wt, rate, res, acc, sq, lam3, mix3, wbuf, xcat, sem):
    depth = o.shape[1]
    copies = [
        pltpu.make_async_copy(
            wt.at[p, chunk_rows(m, depth)], wbuf.at[p, pl.ds(i * depth, depth)], sem.at[2 * p + i]
        )
        for p in range(3)
        for i, m in enumerate((0, 1))
    ]
    wait = run_copies(copies, 4)
    xcat[:, :depth] = o[...]
    xcat[:, depth:] = s[...]
    sq[...] = add_squares(jnp.zeros(sq.shape, jnp.float32), (o, s))
    rates = rate[...]
    lam = jnp.exp(-rates)
    tanh = jnp.tanh(rates)
    mix = res[...] * jnp.sqrt(2.0 * tanh / (1.0 + tanh))

    def put_lam(g, v):
        lam3[:, g, :] = v

    def put_mix(g, v):
        mix3[:, g, :] = v

    by_groups(lam, put_lam)
    by_groups(mix, put_mix)
    for p in range(3):
        wait(2 * p)
        wait(2 * p + 1)
        acc[p] = jnp.dot(xcat[...], wbuf[p], preferred_element_type=jnp.float32)


def second_kernel(x, xs, wt, acc_in, sq_in, acc, sq, cache, wbuf, xcat, sem):
    depth = x.shape[1]
    copies = [
        pltpu.make_async_copy(
            wt.at[p, chunk_rows(m, depth)], wbuf.at[p, pl.ds(i * depth, depth)], sem.at[2 * p + i]
        )
        for p in range(3)
        for i, m in enumerate((2, 3))
    ]
    copies += [
        pltpu.make_async_copy(
            wt.at[1 + p, chunk_rows(m, depth)],
            cache.at[p, pl.ds(i * depth, depth)],
            sem.at[6 + 4 * p + i],
        )
        for p in range(2)
        for i, m in enumerate((4, 6, 5, 7))
    ]
    wait = run_copies(copies, 4)
    xcat[:, :depth] = x[...]
    xcat[:, depth:] = xs[...]
    sq[...] = add_squares(sq_in[...], (x, xs))
    for p in range(3):
        wait(2 * p)
        wait(2 * p + 1)
        acc[p] = acc_in[p] + jnp.dot(xcat[...], wbuf[p], preferred_element_type=jnp.float32)
    for i in range(6, 14):
        wait(i)


def third_kernel(
    y, d, ys, ds, acc_in, sq_in, cache, lam3, docs, xcat, scale, d3, e3
):
    depth = y.shape[1]
    rows = y.shape[0]
    for i, ref in enumerate((y, d, ys, ds)):
        xcat[:, i * depth : (i + 1) * depth] = ref[...]
    total = jnp.sum(add_squares(sq_in[...], (y, d, ys, ds)), axis=1, keepdims=True)
    row = lax.rsqrt(total / (8 * depth) + 1e-06)
    scale[...] = jnp.broadcast_to(row, scale.shape)
    inner = acc_in[1] + jnp.dot(xcat[...], cache[0], preferred_element_type=jnp.float32)
    values = acc_in[2] + jnp.dot(xcat[...], cache[1], preferred_element_type=jnp.float32)
    driven = (inner * row) * (values * row)

    def put(g, v):
        d3[:, g, :] = v

    by_groups(driven, put)
    _, last, _ = own_starts(docs, rows)
    modes = lam3.shape[0]

    def body(step, state):
        for j in range(SUB):
            t = step * SUB + j
            drive = jnp.where(t >= last, d3[t], 0.0)
            state = [lam3[n] * state[n] + drive for n in range(modes)]
        return state

    zeros = [jnp.zeros((SUB, LANE), jnp.float32) for _ in range(modes)]
    state = lax.fori_loop(jnp.maximum(last, 0) // SUB, rows // SUB, body, zeros)
    for n in range(modes):
        e3[n] = state[n]


def own_starts(docs, rows):
    at = -lax.axis_index("ctx") * rows
    first, last, starts = rows, -1, []
    for i in range(docs.shape[0]):
        inside = jnp.logical_and(at >= 0, at < rows)
        first = jnp.where(jnp.logical_and(inside, at < first), at, first)
        last = jnp.where(jnp.logical_and(inside, at > last), at, last)
        starts.append(at)
        at = at + docs[i]
    return first, last, starts


def outer_kernel(xcat, wt, acc_in, d3, lam3, mix3, skip, docs, outer, f3, wbuf, sem):
    rows = xcat.shape[0]
    depth = xcat.shape[1] // 4
    modes = lam3.shape[0]
    copies = [
        pltpu.make_async_copy(
            wt.at[0, chunk_rows(m, depth)], wbuf.at[pl.ds(i * depth, depth)], sem.at[i]
        )
        for i, m in enumerate((4, 6, 5, 7))
    ]
    wait = run_copies(copies, 4)
    _, _, starts = own_starts(docs, rows)

    def body(step, state):
        for j in range(SUB):
            t = step * SUB + j
            begins = starts[0] == t
            for at in starts[1:]:
                begins = jnp.logical_or(begins, at == t)
            keep = jnp.where(begins, 0.0, 1.0)
            drive = d3[t]
            state = [lam3[n] * (state[n] * keep) + drive for n in range(modes)]
            terms = [mix3[n] * state[n] for n in range(modes)]
            while len(terms) > 1:
                terms = [a + b for a, b in zip(terms[::2], terms[1::2])]
            f3[t] = terms[0] + skip[...] * drive
        return state

    zeros = [jnp.zeros((SUB, LANE), jnp.float32) for _ in range(modes)]
    lax.fori_loop(0, rows // SUB, body, zeros)
    for i in range(4):
        wait(i)
    outer[...] = acc_in[0] + jnp.dot(xcat[...], wbuf[...], preferred_element_type=jnp.float32)


def last_kernel(*refs, count):
    arrived = refs[:count]
    outer, f3, scale, lam3, mix3, docs, out = refs[count:]
    rows = outer.shape[0]
    modes = lam3.shape[0]
    first, _, starts = own_starts(docs, rows)
    me = lax.axis_index("ctx")
    begins, valid = [], None
    for k in range(1, count + 1):
        if k > 1:
            inside = [jnp.logical_and(at >= -(k - 1) * rows, at < -(k - 2) * rows) for at in starts]
            clear = jnp.logical_not(functools.reduce(jnp.logical_or, inside))
            valid = jnp.logical_and(jnp.logical_and(valid, clear), me >= k)
        else:
            valid = me >= 1
        begins.append(valid)
    state = []
    for n in range(modes):
        lam = lam3[n]
        whole = lam
        for _ in range(rows.bit_length() - 1):
            whole = whole * whole
        power, total = 1.0, jnp.zeros((SUB, LANE), jnp.float32)
        for k in range(count):
            total = total + jnp.where(begins[k], power * arrived[k][n], 0.0)
            power = power * whole
        state.append(mix3[n] * total)

    def body(step, state):
        for j in range(SUB):
            t = step * SUB + j
            state = [lam3[n] * state[n] for n in range(modes)]
            terms = list(state)
            while len(terms) > 1:
                terms = [a + b for a, b in zip(terms[::2], terms[1::2])]
            f3[t] = f3[t] + jnp.where(t < first, terms[0], 0.0)
        return state

    lax.fori_loop(0, (first + SUB - 1) // SUB, body, state)
    for g in range(SUB):
        cols = slice(g * LANE, (g + 1) * LANE)
        out[:, cols] = (outer[:, cols] * scale[...] * f3[:, g, :]).astype(out.dtype)


def params(mib):
    return pltpu.CompilerParams(vmem_limit_bytes=mib << 20)


def fitted(stream, in_weight, pole_rate, residue, skip_gain, doc_lengths, reach):
    rows, depth = stream.shape
    width, _, local = in_weight.shape
    modes = pole_rate.shape[1]
    size = lax.axis_size("ch")
    wt = jnp.transpose(in_weight, (1, 0, 2))
    rate, res = pole_rate.T, residue.T
    f32, b16 = jnp.float32, jnp.bfloat16
    dma = pltpu.SemaphoreType.DMA

    def swap(block, mask):
        return lax.ppermute(block, "ch", [(i, i ^ mask) for i in range(size)])

    s, x, y, d = (swap(stream, m) for m in (1, 2, 4, 6))
    planes = pltpu.VMEM((3, rows, local), f32)
    squares = pltpu.VMEM((rows, LANE), f32)
    poles = pltpu.VMEM((modes, SUB, LANE), f32)
    cost = functools.partial(pl.CostEstimate, transcendentals=0)
    acc, sq, lam3, mix3 = pl.pallas_call(
        first_kernel,
        in_specs=[IN_VMEM, IN_VMEM, IN_HBM, IN_VMEM, IN_VMEM],
        out_specs=[IN_VMEM] * 4,
        out_shape=[planes, squares, poles, poles],
        scratch_shapes=[
            pltpu.VMEM((3, 2 * depth, local), b16),
            pltpu.VMEM((rows, 2 * depth), b16),
            dma((6,)),
        ],
        compiler_params=params(18),
        cost_estimate=cost(flops=12 * rows * depth * local, bytes_accessed=12 * depth * local),
        name="first",
    )(stream, s, wt, rate, res)
    xs = swap(x, 1)
    acc, sq, cache = pl.pallas_call(
        second_kernel,
        in_specs=[IN_VMEM, IN_VMEM, IN_HBM, IN_VMEM, IN_VMEM],
        out_specs=[IN_VMEM] * 3,
        out_shape=[planes, squares, pltpu.VMEM((2, 4 * depth, local), b16)],
        scratch_shapes=[
            pltpu.VMEM((3, 2 * depth, local), b16),
            pltpu.VMEM((rows, 2 * depth), b16),
            dma((14,)),
        ],
        compiler_params=params(18),
        cost_estimate=cost(flops=12 * rows * depth * local, bytes_accessed=28 * depth * local),
        name="second",
    )(x, xs, wt, acc, sq)
    ys, ds = swap(y, 1), swap(d, 1)
    tokens = pltpu.VMEM((rows, SUB, LANE), f32)
    xcat, scale, d3, e3 = pl.pallas_call(
        third_kernel,
        in_specs=[IN_VMEM] * 8 + [IN_SMEM],
        out_specs=[IN_VMEM] * 4,
        out_shape=[pltpu.VMEM((rows, 4 * depth), b16), squares, tokens, poles],
        compiler_params=params(8),
        cost_estimate=cost(flops=16 * rows * depth * local, bytes_accessed=0),
        name="third",
    )(y, d, ys, ds, acc, sq, cache, lam3, doc_lengths)
    ring = lax.axis_size("ctx")
    arrived = [
        lax.ppermute(e3, "ctx", [(i, (i + k) % ring) for i in range(ring)])
        for k in range(1, reach + 1)
    ]
    outer, f3 = pl.pallas_call(
        outer_kernel,
        in_specs=[IN_VMEM, IN_HBM] + [IN_VMEM] * 5 + [IN_SMEM],
        out_specs=[IN_VMEM] * 2,
        out_shape=[pltpu.VMEM((rows, local), f32), tokens],
        scratch_shapes=[pltpu.VMEM((4 * depth, local), b16), dma((4,))],
        compiler_params=params(14),
        cost_estimate=cost(flops=8 * rows * depth * local, bytes_accessed=8 * depth * local),
        name="outer",
    )(xcat, wt, acc, d3, lam3, mix3, skip_gain.reshape(SUB, LANE), doc_lengths)
    return pl.pallas_call(
        functools.partial(last_kernel, count=reach),
        in_specs=[IN_VMEM] * (reach + 5) + [IN_SMEM],
        out_specs=IN_VMEM,
        out_shape=jax.ShapeDtypeStruct((rows, local), b16),
        compiler_params=params(8),
        name="last",
    )(*arrived, outer, f3, scale, lam3, mix3, doc_lengths)


def solution(mesh):
    placed = (P("ctx", "ch"), P(None, None, "ch"), P("ch", None), P("ch", None), P("ch"), P())
    ring = mesh.shape["ctx"]

    def per_device(*args):
        stream, in_weight = args[0], args[1]
        rows, depth = stream.shape
        longest = rows * ring // 2
        reach = min(ring - 1, (longest + rows - 2) // rows)
        if mesh.shape["ch"] == 8 and in_weight.shape[2] == SUB * LANE and rows == LANE:
            return fitted(*args, reach)
        return general(*args)

    return jax.shard_map(
        per_device, mesh=mesh, in_specs=placed, out_specs=P("ctx", "ch"), check_vma=False
    )
```

profile of v0, /device:TPU:0, one launch (start us, length us, event | category | flops | bytes accessed | tf_op | source)
XLA Modules:
  0.0 50.1 jit_solution(2644870588829918360)
XLA Ops:
  0.0 2.9 %collective-permute-start.4 = (bf16[128,1024]{1,0:T(8,128)(2,1)}, bf16[128,1024]{1,0:T(8,128)(2,1)S(1)}, u32[]{:S(2)}, u32[]{:S(2)}) collective-permute-start(bf16[128,1024]{1,0:T(8,128)(2,1)} %o.1), channel_id=1, source_target_pairs={{0,2},{1,3},{2,0},{3,1},{4,6},{5,7},{6,4},{7,5},{8,10},{9,11},{10,... | collective-permute-start | bytes 786440 | tf_op jit(solution)/shard_map/ppermute | solution.py:306
  2.9 1.5 %collective-permute-start = (bf16[128,1024]{1,0:T(8,128)(2,1)}, bf16[128,1024]{1,0:T(8,128)(2,1)S(1)}, u32[]{:S(2)}, u32[]{:S(2)}) collective-permute-start(bf16[128,1024]{1,0:T(8,128)(2,1)} %o.1), channel_id=1, source_target_pairs={{0,4},{1,5},{2,6},{3,7},{4,0},{5,1},{6,2},{7,3},{8,12},{9,13},{10,... | collective-permute-start | bytes 786440 | tf_op jit(solution)/shard_map/ppermute | solution.py:306
  4.5 0.0 collective-permute-start.1
  4.5 0.0 collective-permute-start.6
  4.5 5.8 %collective-permute-done.4.x = bf16[128,1024]{1,0:T(8,128)(2,1)S(1)} collective-permute-done((bf16[128,1024]{1,0:T(8,128)(2,1)}, bf16[128,1024]{1,0:T(8,128)(2,1)S(1)}, u32[]{:S(2)}, u32[]{:S(2)}) %collective-permute-start.4) | collective-permute-done | bytes 262176 | tf_op jit(solution)/shard_map/ppermute | solution.py:306
  10.3 0.0 collective-permute-start.5
  10.3 6.2 %collective-permute-done.y = bf16[128,1024]{1,0:T(8,128)(2,1)S(1)} collective-permute-done((bf16[128,1024]{1,0:T(8,128)(2,1)}, bf16[128,1024]{1,0:T(8,128)(2,1)S(1)}, u32[]{:S(2)}, u32[]{:S(2)}) %collective-permute-start) | collective-permute-done | bytes 262176 | tf_op jit(solution)/shard_map/ppermute | solution.py:306
  16.5 0.0 collective-permute-start.2
  16.5 0.0 collective-permute-done.1.d
  16.5 0.5 %collective-permute-start.3 = (bf16[128,1024]{1,0:T(8,128)(2,1)S(1)}, bf16[128,1024]{1,0:T(8,128)(2,1)S(1)}, u32[]{:S(2)}, u32[]{:S(2)}) collective-permute-start(bf16[128,1024]{1,0:T(8,128)(2,1)S(1)} %collective-permute-done.1.d), channel_id=1, source_target_pairs={{0,1},{1,0},{2,3},{3,2},{4,5},{5,4},{6,7},{7,6},{8,9},{9,8},{10,11... | collective-permute-start | bytes 786440 | tf_op jit(solution)/shard_map/ppermute | solution.py:306
  17.0 0.0 collective-permute-done.6.s
  17.1 0.0 copy-start
  17.1 0.9 %copy-done = bf16[128,1024]{1,0:T(8,128)(2,1)S(1)} copy-done((bf16[128,1024]{1,0:T(8,128)(2,1)S(1)}, bf16[128,1024]{1,0:T(8,128)(2,1)}, u32[]{:S(2)}) %copy-start) | copy-done | bytes 262168
  18.0 0.0 copy-start.1
  18.0 0.8 %copy-done.1 = f32[1024,16]{0,1:T(8,128)S(1)} copy-done((f32[1024,16]{0,1:T(8,128)S(1)}, f32[1024,16]{0,1:T(8,128)}, u32[]{:S(2)}) %copy-start.1) | copy-done | bytes 65560
  18.8 0.0 copy-start.2
  18.8 0.8 %copy-done.2 = f32[1024,16]{0,1:T(8,128)S(1)} copy-done((f32[1024,16]{0,1:T(8,128)S(1)}, f32[1024,16]{0,1:T(8,128)}, u32[]{:S(2)}) %copy-start.2) | copy-done | bytes 65560
  19.7 5.7 %first.1 = (f32[3,128,1024]{2,1,0:T(8,128)S(1)}, f32[128,128]{1,0:T(8,128)S(1)}, f32[16,8,128]{2,1,0:T(8,128)S(1)}, f32[16,8,128]{2,1,0:T(8,128)S(1)}) custom-call(bf16[128,1024]{1,0:T(8,128)(2,1)S(1)} %copy-done, bf16[128,1024]{1,0:T(8,128)(2,1)S(1)} %collective-permute-done.6.s, bf16[3,8192,1024]{2,1,0:T(8,128)(2,1)} %bitcast.7, f32[16,1024]{1,0:T(8,128)S(1)} %bitcast.4, ...), custom_call_target="tpu_custom_call" | custom-call | flops 1610612736 | bytes 12582912 | tf_op jit(solution)/shard_map/first/pallas_call | solution.py:313
  25.4 0.0 collective-permute-done.5.xs
  25.4 0.0 copy-start.3
  25.4 9.8 %second.1 = (f32[3,128,1024]{2,1,0:T(8,128)S(1)}, f32[128,128]{1,0:T(8,128)S(1)}, bf16[2,4096,1024]{2,1,0:T(8,128)(2,1)S(1)}) custom-call(bf16[128,1024]{1,0:T(8,128)(2,1)S(1)} %collective-permute-done.4.x, bf16[128,1024]{1,0:T(8,128)(2,1)S(1)} %collective-permute-done.5.xs, bf16[3,8192,1024]{2,1,0:T(8,128)(2,1)} %bitcast.8, ...), custom_call_target="tpu_custom_call" | custom-call | flops 1610612736 | bytes 29360128 | tf_op jit(solution)/shard_map/second/pallas_call | solution.py:328
  35.2 0.0 copy-start.4
  35.2 0.0 collective-permute-done.2.ys
  35.2 0.0 collective-permute-done.3.ds
  35.2 0.0 copy-done.3
  35.2 3.8 %third.1 = (bf16[128,4096]{1,0:T(8,128)(2,1)S(1)}, f32[128,128]{1,0:T(8,128)S(1)}, f32[128,8,128]{2,1,0:T(8,128)S(1)}, f32[16,8,128]{2,1,0:T(8,128)S(1)}) custom-call(bf16[128,1024]{1,0:T(8,128)(2,1)S(1)} %collective-permute-done.y, bf16[128,1024]{1,0:T(8,128)(2,1)S(1)} %collective-permute-done.1.d, bf16[128,1024]{1,0:T(8,128)(2,1)S(1)} %collective-permute-done.2.ys, ...), custom_call_target="tpu_custom_call" | custom-call | flops 2147483648 | tf_op jit(solution)/shard_map/third/pallas_call | solution.py:344
  39.0 1.6 %collective-permute-start.7 = (f32[16,8,128]{2,1,0:T(8,128)S(1)}, f32[16,8,128]{2,1,0:T(8,128)S(1)}, u32[]{:S(2)}, u32[]{:S(2)}) collective-permute-start(f32[16,8,128]{2,1,0:T(8,128)S(1)} %get-tuple-element.24), channel_id=1, source_target_pairs={{0,8},{8,16},{16,24},{24,0},{1,9},{9,17},{17,25},{25,1},{2,10},{10... | collective-permute-start | bytes 196616 | tf_op jit(solution)/shard_map/ppermute | solution.py:355
  40.6 2.5 %collective-permute-start.8 = (f32[16,8,128]{2,1,0:T(8,128)S(1)}, f32[16,8,128]{2,1,0:T(8,128)S(1)}, u32[]{:S(2)}, u32[]{:S(2)}) collective-permute-start(f32[16,8,128]{2,1,0:T(8,128)S(1)} %get-tuple-element.24), channel_id=1, source_target_pairs={{0,16},{8,24},{16,0},{24,8},{1,17},{9,25},{17,1},{25,9},{2,18},{10... | collective-permute-start | bytes 196616 | tf_op jit(solution)/shard_map/ppermute | solution.py:355
  43.1 0.0 copy-done.4
  43.1 5.3 %outer.1 = (f32[128,1024]{1,0:T(8,128)S(1)}, f32[128,8,128]{2,1,0:T(8,128)S(1)}) custom-call(bf16[128,4096]{1,0:T(8,128)(2,1)S(1)} %get-tuple-element.25.xcat, bf16[3,8192,1024]{2,1,0:T(8,128)(2,1)} %bitcast.9, f32[3,128,1024]{2,1,0:T(8,128)S(1)} %get-tuple-element.20.acc_in, f32[128,8,128]{2,1,0:T(8,128)S(1)} %get-tuple-element.26.d3, ...), custom_call_target="tpu_custom_call" | custom-call | flops 1073741824 | bytes 8388608 | tf_op jit(solution)/shard_map/outer/pallas_call | solution.py:358
  48.4 0.0 collective-permute-done.7.refs_0_
  48.4 0.0 collective-permute-done.8.refs_1_
  48.5 1.6 %last.1 = bf16[128,1024]{1,0:T(8,128)(2,1)} custom-call(f32[16,8,128]{2,1,0:T(8,128)S(1)} %collective-permute-done.7.refs_0_, f32[16,8,128]{2,1,0:T(8,128)S(1)} %collective-permute-done.8.refs_1_, f32[128,1024]{1,0:T(8,128)S(1)} %get-tuple-element.28.refs_2_, f32[128,8,128]{2,1,0:T(8,128)S(1)} %get-tuple-element.29.refs_3_, ...), custom_call_target="tpu_custom_call" | custom-call | tf_op jit(solution)/shard_map/last/pallas_call | solution.py:368
Async XLA Ops:
  0.0 10.3 %collective-permute-start.4 = (bf16[128,1024]{1,0:T(8,128)(2,1)}, bf16[128,1024]{1,0:T(8,128)(2,1)S(1)}, u32[]{:S(2)}, u32[]{:S(2)}) collective-permute-start(bf16[128,1024]{1,0:T(8,128)(2,1)} %o.1), channel_id=1, source_target_pairs={{0,2},{1,3},{2,0},{3,1},{4,6},{5,7},{6,4},{7,5},{8,10},{9,11},{10,... | collective-permute-start | bytes 786440 | tf_op jit(solution)/shard_map/ppermute | solution.py:306
  2.9 13.6 %collective-permute-start = (bf16[128,1024]{1,0:T(8,128)(2,1)}, bf16[128,1024]{1,0:T(8,128)(2,1)S(1)}, u32[]{:S(2)}, u32[]{:S(2)}) collective-permute-start(bf16[128,1024]{1,0:T(8,128)(2,1)} %o.1), channel_id=1, source_target_pairs={{0,4},{1,5},{2,6},{3,7},{4,0},{5,1},{6,2},{7,3},{8,12},{9,13},{10,... | collective-permute-start | bytes 786440 | tf_op jit(solution)/shard_map/ppermute | solution.py:306
  4.5 12.1 %collective-permute-start.1 = (bf16[128,1024]{1,0:T(8,128)(2,1)}, bf16[128,1024]{1,0:T(8,128)(2,1)S(1)}, u32[]{:S(2)}, u32[]{:S(2)}) collective-permute-start(bf16[128,1024]{1,0:T(8,128)(2,1)} %o.1), channel_id=1, source_target_pairs={{0,6},{1,7},{2,4},{3,5},{4,2},{5,3},{6,0},{7,1},{8,14},{9,15},{10,... | collective-permute-start | bytes 786440 | tf_op jit(solution)/shard_map/ppermute | solution.py:306
  4.5 12.6 %collective-permute-start.6 = (bf16[128,1024]{1,0:T(8,128)(2,1)}, bf16[128,1024]{1,0:T(8,128)(2,1)S(1)}, u32[]{:S(2)}, u32[]{:S(2)}) collective-permute-start(bf16[128,1024]{1,0:T(8,128)(2,1)} %o.1), channel_id=1, source_target_pairs={{0,1},{1,0},{2,3},{3,2},{4,5},{5,4},{6,7},{7,6},{8,9},{9,8},{10,11... | collective-permute-start | bytes 786440 | tf_op jit(solution)/shard_map/ppermute | solution.py:306
  10.3 15.1 %collective-permute-start.5 = (bf16[128,1024]{1,0:T(8,128)(2,1)S(1)}, bf16[128,1024]{1,0:T(8,128)(2,1)S(1)}, u32[]{:S(2)}, u32[]{:S(2)}) collective-permute-start(bf16[128,1024]{1,0:T(8,128)(2,1)S(1)} %collective-permute-done.4.x), channel_id=1, source_target_pairs={{0,1},{1,0},{2,3},{3,2},{4,5},{5,4},{6,7},{7,6},{8,9},{9,8},{10,11... | collective-permute-start | bytes 786440 | tf_op jit(solution)/shard_map/ppermute | solution.py:306
  16.5 18.7 %collective-permute-start.2 = (bf16[128,1024]{1,0:T(8,128)(2,1)S(1)}, bf16[128,1024]{1,0:T(8,128)(2,1)S(1)}, u32[]{:S(2)}, u32[]{:S(2)}) collective-permute-start(bf16[128,1024]{1,0:T(8,128)(2,1)S(1)} %collective-permute-done.y), channel_id=1, source_target_pairs={{0,1},{1,0},{2,3},{3,2},{4,5},{5,4},{6,7},{7,6},{8,9},{9,8},{10,11... | collective-permute-start | bytes 786440 | tf_op jit(solution)/shard_map/ppermute | solution.py:306
  16.5 18.7 %collective-permute-start.3 = (bf16[128,1024]{1,0:T(8,128)(2,1)S(1)}, bf16[128,1024]{1,0:T(8,128)(2,1)S(1)}, u32[]{:S(2)}, u32[]{:S(2)}) collective-permute-start(bf16[128,1024]{1,0:T(8,128)(2,1)S(1)} %collective-permute-done.1.d), channel_id=1, source_target_pairs={{0,1},{1,0},{2,3},{3,2},{4,5},{5,4},{6,7},{7,6},{8,9},{9,8},{10,11... | collective-permute-start | bytes 786440 | tf_op jit(solution)/shard_map/ppermute | solution.py:306
  17.1 1.0 %copy-start = (bf16[128,1024]{1,0:T(8,128)(2,1)S(1)}, bf16[128,1024]{1,0:T(8,128)(2,1)}, u32[]{:S(2)}) copy-start(bf16[128,1024]{1,0:T(8,128)(2,1)} %o.1) | copy-start | bytes 786436
  18.0 0.8 %copy-start.1 = (f32[1024,16]{0,1:T(8,128)S(1)}, f32[1024,16]{0,1:T(8,128)}, u32[]{:S(2)}) copy-start(f32[1024,16]{0,1:T(8,128)} %param.8) | copy-start | bytes 196612
  18.8 0.8 %copy-start.2 = (f32[1024,16]{0,1:T(8,128)S(1)}, f32[1024,16]{0,1:T(8,128)}, u32[]{:S(2)}) copy-start(f32[1024,16]{0,1:T(8,128)} %param.9) | copy-start | bytes 196612
  25.4 9.9 %copy-start.3 = (s32[8]{0:T(128)S(1)}, s32[8]{0:T(128)}, u32[]{:S(2)}) copy-start(s32[8]{0:T(128)} %refs_7_.1) | copy-start | bytes 100
  35.2 7.9 %copy-start.4 = (f32[1024]{0:T(1024)S(1)}, f32[1024]{0:T(1024)}, u32[]{:S(2)}) copy-start(f32[1024]{0:T(1024)} %param.10) | copy-start | bytes 12292
  39.0 9.4 %collective-permute-start.7 = (f32[16,8,128]{2,1,0:T(8,128)S(1)}, f32[16,8,128]{2,1,0:T(8,128)S(1)}, u32[]{:S(2)}, u32[]{:S(2)}) collective-permute-start(f32[16,8,128]{2,1,0:T(8,128)S(1)} %get-tuple-element.24), channel_id=1, source_target_pairs={{0,8},{8,16},{16,24},{24,0},{1,9},{9,17},{17,25},{25,1},{2,10},{10... | collective-permute-start | bytes 196616 | tf_op jit(solution)/shard_map/ppermute | solution.py:355
  40.6 7.9 %collective-permute-start.8 = (f32[16,8,128]{2,1,0:T(8,128)S(1)}, f32[16,8,128]{2,1,0:T(8,128)S(1)}, u32[]{:S(2)}, u32[]{:S(2)}) collective-permute-start(f32[16,8,128]{2,1,0:T(8,128)S(1)} %get-tuple-element.24), channel_id=1, source_target_pairs={{0,16},{8,24},{16,0},{24,8},{1,17},{9,25},{17,1},{25,9},{2,18},{10... | collective-permute-start | bytes 196616 | tf_op jit(solution)/shard_map/ppermute | solution.py:355
where the time goes:
time: 50.3 us; the launch traced here: 50.1 us
  Pallas kernels  26.2 us (52%)
  waiting for transfers between devices  12.1 us (24%)
  starting transfers between devices  9.02 us (18%)
  local copies, waits for them, and re-layouts  2.64 us (5%)
    ppermute x7, waiting for transfers between devices, swap(): return lax.ppermute(block, 'ch', [(i, i ^ mask) for i in range(size)])  12.1 us
    pallas_call x1, Pallas kernels, fitted(): pl.pallas_call(second_kernel, in_specs=[IN_VMEM, IN_VMEM, IN_HBM, IN_VMEM...  9.8 us
    pallas_call x1, Pallas kernels, fitted(): pl.pallas_call(first_kernel, in_specs=[IN_VMEM, IN_VMEM, IN_HBM, IN_VMEM,...  5.66 us
    pallas_call x1, Pallas kernels, fitted(): pl.pallas_call(outer_kernel, in_specs=[IN_VMEM, IN_HBM] + [IN_VMEM] * 5 +...  5.33 us
    ppermute x7, starting transfers between devices, swap(): return lax.ppermute(block, 'ch', [(i, i ^ mask) for i in range(size)])  4.98 us
    ppermute x2, starting transfers between devices, fitted(): lax.ppermute(e3, 'ctx', [(i, (i + k) % ring) for i in range(ring)])  4.04 us
    pallas_call x1, Pallas kernels, fitted(): pl.pallas_call(third_kernel, in_specs=[IN_VMEM] * 8 + [IN_SMEM], out_spec...  3.81 us
    unnamed x10, local copies, waits for them, and re-layouts  2.64 us
  transfers between devices with their start and end apart: 9, of which 2 were waited for; matrix products, arithmetic and copies ran while one was open for 0% of the time, Pallas kernels for 42%

commit v1 on v0

--- a/solution.py
+++ b/solution.py
@@ -10,8 +10,10 @@
 SUB = 8
 LANE = 128
 IN_VMEM = pl.BlockSpec(memory_space=pltpu.VMEM)
+IN_HBM = pl.BlockSpec(memory_space=pltpu.HBM)
 IN_SMEM = pl.BlockSpec(memory_space=pltpu.SMEM)
-IN_HBM = pl.BlockSpec(memory_space=pl.ANY)
+DRIVEN = (1, 2)
+GATE = (0,)
 
 
 def shifted(block, axis, distance):
@@ -84,6 +86,15 @@
     return total
 
 
+def by_groups(value, store):
+    for g in range(SUB):
+        store(g, value[:, g * LANE : (g + 1) * LANE])
+
+
+def dot(a, b):
+    return jnp.dot(a, b, preferred_element_type=jnp.float32)
+
+
 def run_copies(copies, ahead):
     for c in copies[:ahead]:
         c.start()
@@ -96,28 +107,61 @@
     return wait
 
 
-def by_groups(value, store):
-    for g in range(SUB):
-        store(g, value[:, g * LANE : (g + 1) * LANE])
-
-
-def first_kernel(o, s, wt, rate, res, acc, sq, lam3, mix3, wbuf, xcat, sem):
-    depth = o.shape[1]
-    copies = [
+def weight_copies(wt, planes, masks, depth, target, sem, at=0):
+    return [
         pltpu.make_async_copy(
-            wt.at[p, chunk_rows(m, depth)], wbuf.at[p, pl.ds(i * depth, depth)], sem.at[2 * p + i]
+            wt.at[p, chunk_rows(m, depth)],
+            target.at[k, pl.ds(i * depth, depth)],
+            sem.at[at + k * len(masks) + i],
         )
-        for p in range(3)
-        for i, m in enumerate((0, 1))
+        for k, p in enumerate(planes)
+        for i, m in enumerate(masks)
     ]
-    wait = run_copies(copies, 4)
-    xcat[:, :depth] = o[...]
-    xcat[:, depth:] = s[...]
-    sq[...] = add_squares(jnp.zeros(sq.shape, jnp.float32), (o, s))
-    rates = rate[...]
-    lam = jnp.exp(-rates)
-    tanh = jnp.tanh(rates)
-    mix = res[...] * jnp.sqrt(2.0 * tanh / (1.0 + tanh))
+
+
+def project(blocks, weights, plane):
+    depth = blocks[0].shape[1]
+    total = dot(blocks[0][...], weights[plane, :depth])
+    for i in range(1, len(blocks)):
+        total = total + dot(blocks[i][...], weights[plane, i * depth : (i + 1) * depth])
+    return total
+
+
+def own_masks():
+    core = lax.axis_index("ch") & 1
+    one, two = 2 + 2 * core, 4 - 2 * core
+    return (one, two, 6)
+
+
+def other_masks():
+    core = lax.axis_index("ch") & 1
+    one, two = 2 + 2 * core, 4 - 2 * core
+    return (two ^ 1, one ^ 1, 7)
+
+
+def first_kernel(
+    o, s, wt, rate, res, acc, sq, lam3, mix3, held, near, far, wbuf, rates, ress, sem, small
+):
+    depth = s.shape[1]
+    own = [
+        pltpu.make_async_copy(o, held, small.at[0]),
+        pltpu.make_async_copy(rate, rates, small.at[1]),
+        pltpu.make_async_copy(res, ress, small.at[2]),
+    ]
+    for c in own:
+        c.start()
+    copies = weight_copies(wt, DRIVEN, (0, 1), depth, wbuf, sem)
+    copies += weight_copies(wt, DRIVEN, own_masks(), depth, near, sem, 4)
+    copies += weight_copies(wt, DRIVEN, other_masks(), depth, far, sem, 10)
+    wait = run_copies(copies, 8)
+    for c in own:
+        c.wait()
+    blocks = (held, s)
+    sq[...] = add_squares(jnp.zeros(sq.shape, jnp.float32), blocks)
+    r = rates[...]
+    lam = jnp.exp(-r)
+    tanh = jnp.tanh(r)
+    mix = ress[...] * jnp.sqrt(2.0 * tanh / (1.0 + tanh))
 
     def put_lam(g, v):
         lam3[:, g, :] = v
@@ -127,54 +171,30 @@
 
     by_groups(lam, put_lam)
     by_groups(mix, put_mix)
-    for p in range(3):
-        wait(2 * p)
-        wait(2 * p + 1)
-        acc[p] = jnp.dot(xcat[...], wbuf[p], preferred_element_type=jnp.float32)
-
-
-def second_kernel(x, xs, wt, acc_in, sq_in, acc, sq, cache, wbuf, xcat, sem):
-    depth = x.shape[1]
-    copies = [
-        pltpu.make_async_copy(
-            wt.at[p, chunk_rows(m, depth)], wbuf.at[p, pl.ds(i * depth, depth)], sem.at[2 * p + i]
-        )
-        for p in range(3)
-        for i, m in enumerate((2, 3))
-    ]
-    copies += [
-        pltpu.make_async_copy(
-            wt.at[1 + p, chunk_rows(m, depth)],
-            cache.at[p, pl.ds(i * depth, depth)],
-            sem.at[6 + 4 * p + i],
-        )
-        for p in range(2)
-        for i, m in enumerate((4, 6, 5, 7))
-    ]
-    wait = run_copies(copies, 4)
-    xcat[:, :depth] = x[...]
-    xcat[:, depth:] = xs[...]
-    sq[...] = add_squares(sq_in[...], (x, xs))
-    for p in range(3):
-        wait(2 * p)
-        wait(2 * p + 1)
-        acc[p] = acc_in[p] + jnp.dot(xcat[...], wbuf[p], preferred_element_type=jnp.float32)
-    for i in range(6, 14):
+    for k in range(2):
+        wait(2 * k)
+        wait(2 * k + 1)
+        acc[k] = project(blocks, wbuf, k)
+    for i in range(4, len(copies)):
         wait(i)
 
 
-def third_kernel(
-    y, d, ys, ds, acc_in, sq_in, cache, lam3, docs, xcat, scale, d3, e3
-):
-    depth = y.shape[1]
-    rows = y.shape[0]
-    for i, ref in enumerate((y, d, ys, ds)):
-        xcat[:, i * depth : (i + 1) * depth] = ref[...]
-    total = jnp.sum(add_squares(sq_in[...], (y, d, ys, ds)), axis=1, keepdims=True)
+def near_kernel(a, b, d, weights, acc_in, sq_in, acc, sq):
+    blocks = (a, b, d)
+    sq[...] = add_squares(sq_in[...], blocks)
+    for k in range(2):
+        acc[k] = acc_in[k] + project(blocks, weights, k)
+
+
+def far_kernel(a, b, d, weights, wt, acc_in, sq_in, lam3, docs, scale, d3, e3, gate, sem):
+    rows, depth = a.shape
+    wait = run_copies(weight_copies(wt, GATE, (0, 1), depth, gate, sem), 8)
+    blocks = (a, b, d)
+    total = jnp.sum(add_squares(sq_in[...], blocks), axis=1, keepdims=True)
     row = lax.rsqrt(total / (8 * depth) + 1e-06)
     scale[...] = jnp.broadcast_to(row, scale.shape)
-    inner = acc_in[1] + jnp.dot(xcat[...], cache[0], preferred_element_type=jnp.float32)
-    values = acc_in[2] + jnp.dot(xcat[...], cache[1], preferred_element_type=jnp.float32)
+    inner = acc_in[0] + project(blocks, weights, 0)
+    values = acc_in[1] + project(blocks, weights, 1)
     driven = (inner * row) * (values * row)
 
     def put(g, v):
@@ -195,6 +215,8 @@
     state = lax.fori_loop(jnp.maximum(last, 0) // SUB, rows // SUB, body, zeros)
     for n in range(modes):
         e3[n] = state[n]
+    for i in range(2):
+        wait(i)
 
 
 def own_starts(docs, rows):
@@ -209,17 +231,13 @@
     return first, last, starts
 
 
-def outer_kernel(xcat, wt, acc_in, d3, lam3, mix3, skip, docs, outer, f3, wbuf, sem):
-    rows = xcat.shape[0]
-    depth = xcat.shape[1] // 4
+def outer_kernel(
+    o, s, a, b, d, ao, bo, do, wt, gate, d3, lam3, mix3, skip, docs, outer, f3, wbuf, sem
+):
+    rows, depth = o.shape
+    masks = own_masks() + other_masks()
+    wait = run_copies(weight_copies(wt, GATE, masks, depth, wbuf, sem), 8)
     modes = lam3.shape[0]
-    copies = [
-        pltpu.make_async_copy(
-            wt.at[0, chunk_rows(m, depth)], wbuf.at[pl.ds(i * depth, depth)], sem.at[i]
-        )
-        for i, m in enumerate((4, 6, 5, 7))
-    ]
-    wait = run_copies(copies, 4)
     _, _, starts = own_starts(docs, rows)
 
     def body(step, state):
@@ -233,15 +251,17 @@
             state = [lam3[n] * (state[n] * keep) + drive for n in range(modes)]
             terms = [mix3[n] * state[n] for n in range(modes)]
             while len(terms) > 1:
-                terms = [a + b for a, b in zip(terms[::2], terms[1::2])]
+                terms = [p + q for p, q in zip(terms[::2], terms[1::2])]
             f3[t] = terms[0] + skip[...] * drive
         return state
 
     zeros = [jnp.zeros((SUB, LANE), jnp.float32) for _ in range(modes)]
     lax.fori_loop(0, rows // SUB, body, zeros)
-    for i in range(4):
+    total = project((o, s), gate, 0)
+    for i, block in enumerate((a, b, d, ao, bo, do)):
         wait(i)
-    outer[...] = acc_in[0] + jnp.dot(xcat[...], wbuf[...], preferred_element_type=jnp.float32)
+        total = total + dot(block[...], wbuf[0, i * depth : (i + 1) * depth])
+    outer[...] = total
 
 
 def last_kernel(*refs, count):
@@ -305,66 +325,77 @@
     def swap(block, mask):
         return lax.ppermute(block, "ch", [(i, i ^ mask) for i in range(size)])
 
-    s, x, y, d = (swap(stream, m) for m in (1, 2, 4, 6))
-    planes = pltpu.VMEM((3, rows, local), f32)
+    def split(block, first):
+        masks = (2, 4) if first else (4, 2)
+        return lax.ppermute(block, "ch", [(i, i ^ masks[i & 1]) for i in range(size)])
+
+    def call(kernel, ins, outs, scratch, flops, mib):
+        return pl.pallas_call(
+            kernel,
+            in_specs=[spec for spec, _ in ins],
+            out_specs=[IN_VMEM] * len(outs),
+            out_shape=outs,
+            scratch_shapes=scratch,
+            compiler_params=params(mib),
+            cost_estimate=pl.CostEstimate(
+                flops=2 * rows * depth * local * flops, bytes_accessed=0, transcendentals=0
+            ),
+            name=kernel.__name__,
+        )(*[array for _, array in ins])
+
+    def here(*arrays):
+        return [(IN_VMEM, a) for a in arrays]
+
+    planes = pltpu.VMEM((2, rows, local), f32)
     squares = pltpu.VMEM((rows, LANE), f32)
     poles = pltpu.VMEM((modes, SUB, LANE), f32)
-    cost = functools.partial(pl.CostEstimate, transcendentals=0)
-    acc, sq, lam3, mix3 = pl.pallas_call(
+    tokens = pltpu.VMEM((rows, SUB, LANE), f32)
+    chunk = pltpu.VMEM((rows, depth), b16)
+    vector = pltpu.VMEM((modes, local), f32)
+
+    def there(*arrays):
+        return [(IN_HBM, pltpu.with_memory_space_constraint(a, pltpu.HBM)) for a in arrays]
+
+    def weights(planes_of, chunks):
+        return pltpu.VMEM((planes_of, chunks * depth, local), b16)
+
+    s = swap(stream, 1)
+    a, b, d = split(stream, True), split(stream, False), swap(stream, 6)
+    acc, sq, lam3, mix3, o, near, far = call(
         first_kernel,
-        in_specs=[IN_VMEM, IN_VMEM, IN_HBM, IN_VMEM, IN_VMEM],
-        out_specs=[IN_VMEM] * 4,
-        out_shape=[planes, squares, poles, poles],
-        scratch_shapes=[
-            pltpu.VMEM((3, 2 * depth, local), b16),
-            pltpu.VMEM((rows, 2 * depth), b16),
-            dma((6,)),
-        ],
-        compiler_params=params(18),
-        cost_estimate=cost(flops=12 * rows * depth * local, bytes_accessed=12 * depth * local),
-        name="first",
-    )(stream, s, wt, rate, res)
-    xs = swap(x, 1)
-    acc, sq, cache = pl.pallas_call(
-        second_kernel,
-        in_specs=[IN_VMEM, IN_VMEM, IN_HBM, IN_VMEM, IN_VMEM],
-        out_specs=[IN_VMEM] * 3,
-        out_shape=[planes, squares, pltpu.VMEM((2, 4 * depth, local), b16)],
-        scratch_shapes=[
-            pltpu.VMEM((3, 2 * depth, local), b16),
-            pltpu.VMEM((rows, 2 * depth), b16),
-            dma((14,)),
-        ],
-        compiler_params=params(18),
-        cost_estimate=cost(flops=12 * rows * depth * local, bytes_accessed=28 * depth * local),
-        name="second",
-    )(x, xs, wt, acc, sq)
-    ys, ds = swap(y, 1), swap(d, 1)
-    tokens = pltpu.VMEM((rows, SUB, LANE), f32)
-    xcat, scale, d3, e3 = pl.pallas_call(
-        third_kernel,
-        in_specs=[IN_VMEM] * 8 + [IN_SMEM],
-        out_specs=[IN_VMEM] * 4,
-        out_shape=[pltpu.VMEM((rows, 4 * depth), b16), squares, tokens, poles],
-        compiler_params=params(8),
-        cost_estimate=cost(flops=16 * rows * depth * local, bytes_accessed=0),
-        name="third",
-    )(y, d, ys, ds, acc, sq, cache, lam3, doc_lengths)
+        there(stream) + here(s) + there(wt, rate, res),
+        [planes, squares, poles, poles, chunk, weights(2, 3), weights(2, 3)],
+        [weights(2, 2), vector, vector, dma((16,)), dma((3,))],
+        4,
+        12,
+    )
+    a, b, d, acc, sq = lax.optimization_barrier((a, b, d, acc, sq))
+    ao, bo, do = swap(a, 1), swap(b, 1), swap(d, 1)
+    acc, sq = call(near_kernel, here(a, b, d, near, acc, sq), [planes, squares], [], 6, 4)
+    scale, d3, e3, gate = call(
+        far_kernel,
+        here(ao, bo, do, far) + there(wt) + here(acc, sq, lam3) + [(IN_SMEM, doc_lengths)],
+        [squares, tokens, poles, weights(1, 2)],
+        [dma((2,))],
+        6,
+        4,
+    )
     ring = lax.axis_size("ctx")
     arrived = [
         lax.ppermute(e3, "ctx", [(i, (i + k) % ring) for i in range(ring)])
         for k in range(1, reach + 1)
     ]
-    outer, f3 = pl.pallas_call(
+    outer, f3 = call(
         outer_kernel,
-        in_specs=[IN_VMEM, IN_HBM] + [IN_VMEM] * 5 + [IN_SMEM],
-        out_specs=[IN_VMEM] * 2,
-        out_shape=[pltpu.VMEM((rows, local), f32), tokens],
-        scratch_shapes=[pltpu.VMEM((4 * depth, local), b16), dma((4,))],
-        compiler_params=params(14),
-        cost_estimate=cost(flops=8 * rows * depth * local, bytes_accessed=8 * depth * local),
-        name="outer",
-    )(xcat, wt, acc, d3, lam3, mix3, skip_gain.reshape(SUB, LANE), doc_lengths)
+        here(o, s, a, b, d, ao, bo, do)
+        + there(wt)
+        + here(gate, d3, lam3, mix3, skip_gain.reshape(SUB, LANE))
+        + [(IN_SMEM, doc_lengths)],
+        [pltpu.VMEM((rows, local), f32), tokens],
+        [weights(1, 6), dma((6,))],
+        8,
+        16,
+    )
     return pl.pallas_call(
         functools.partial(last_kernel, count=reach),
         in_specs=[IN_VMEM] * (reach + 5) + [IN_SMEM],

time: 50.3 us -> 36 us (0.72)
  waiting for transfers between devices: 12.1 us -> 0.83 us
  local copies, waits for them, and re-layouts: 2.64 us -> 0.01 us
  Pallas kernels: 26.2 us -> 25.6 us
    ppermute x7 -> x5, waiting for transfers between devices: 12.1 us -> 0.01 us  [swap(): return lax.ppermute(block, 'ch', [(i, i ^ mask) for i in range(size)])]
    unnamed x10 -> x4, local copies, waits for them, and re-layouts: 2.64 us -> 0.01 us
    ppermute x0 -> x2, waiting for transfers between devices: none -> 0.82 us  [split(): lax.ppermute(block, 'ch', [(i, i ^ masks[i & 1]) for i in range(size)])]
    pallas_call x4, Pallas kernels: 24.6 us -> 24 us  [call(): pl.pallas_call(kernel, in_specs=[spec for spec, _ in ins], out_specs=[IN_...]
    ppermute x0 -> x2, starting transfers between devices: none -> 0.63 us  [split(): lax.ppermute(block, 'ch', [(i, i ^ masks[i & 1]) for i in range(size)])]
    ppermute x7 -> x5, starting transfers between devices: 4.98 us -> 4.41 us  [swap(): return lax.ppermute(block, 'ch', [(i, i ^ mask) for i in range(size)])]
  transfers between devices with their start and end apart: 9 -> 9, of which waited for: 2 -> 2; matrix products, arithmetic and copies ran while one was open for 0% -> 0% of each run, Pallas kernels for 42% -> 54%
where the time goes in v1:
time: 36 us; the launch traced here: 35.8 us
  Pallas kernels  25.6 us (71%)
  starting transfers between devices  9.27 us (26%)
  waiting for transfers between devices  0.83 us (2%)
    pallas_call x4, Pallas kernels, call(): pl.pallas_call(kernel, in_specs=[spec for spec, _ in ins], out_specs=[IN_...  24 us
    ppermute x5, starting transfers between devices, swap(): return lax.ppermute(block, 'ch', [(i, i ^ mask) for i in range(size)])  4.41 us
    ppermute x2, starting transfers between devices, fitted(): lax.ppermute(e3, 'ctx', [(i, (i + k) % ring) for i in range(ring)])  4.22 us
    pallas_call x1, Pallas kernels, fitted(): pl.pallas_call(functools.partial(last_kernel, count=reach), in_specs=[IN_...  1.65 us
    ppermute x2, waiting for transfers between devices, split(): lax.ppermute(block, 'ch', [(i, i ^ masks[i & 1]) for i in range(size)])  0.82 us
  transfers between devices with their start and end apart: 9, of which 2 were waited for; matrix products, arithmetic and copies ran while one was open for 0% of the time, Pallas kernels for 54%

profile of v1, /device:TPU:0, one launch (start us, length us, event | category | flops | bytes accessed | tf_op | source)
XLA Modules:
  0.0 35.8 jit_solution(16821902214399941596)
XLA Ops:
  0.0 0.5 %collective-permute-start.3 = (bf16[128,1024]{1,0:T(8,128)(2,1)}, bf16[128,1024]{1,0:T(8,128)(2,1)S(1)}, u32[]{:S(2)}, u32[]{:S(2)}) collective-permute-start(bf16[128,1024]{1,0:T(8,128)(2,1)} %o.1), channel_id=1, source_target_pairs={{0,1},{1,0},{2,3},{3,2},{4,5},{5,4},{6,7},{7,6},{8,9},{9,8},{10,11... | collective-permute-start | bytes 786440 | tf_op jit(solution)/shard_map/ppermute | solution.py:326
  0.5 3.4 %collective-permute-start.2 = (bf16[128,1024]{1,0:T(8,128)(2,1)}, bf16[128,1024]{1,0:T(8,128)(2,1)S(1)}, u32[]{:S(2)}, u32[]{:S(2)}) collective-permute-start(bf16[128,1024]{1,0:T(8,128)(2,1)} %o.1), channel_id=1, source_target_pairs={{0,6},{1,7},{2,4},{3,5},{4,2},{5,3},{6,0},{7,1},{8,14},{9,15},{10,... | collective-permute-start | bytes 786440 | tf_op jit(solution)/shard_map/ppermute | solution.py:326
  3.9 0.5 %collective-permute-start.1 = (bf16[128,1024]{1,0:T(8,128)(2,1)}, bf16[128,1024]{1,0:T(8,128)(2,1)S(1)}, u32[]{:S(2)}, u32[]{:S(2)}) collective-permute-start(bf16[128,1024]{1,0:T(8,128)(2,1)} %o.1), channel_id=1, source_target_pairs={{0,4},{1,3},{2,6},{3,1},{4,0},{5,7},{6,2},{7,5},{8,12},{9,11},{10,... | collective-permute-start | bytes 786440 | tf_op jit(solution)/shard_map/ppermute | solution.py:330
  4.4 0.1 collective-permute-start
  4.5 0.0 collective-permute-done.3.s
  4.5 11.6 %first_kernel.1 = (f32[2,128,1024]{2,1,0:T(8,128)S(1)}, f32[128,128]{1,0:T(8,128)S(1)}, f32[16,8,128]{2,1,0:T(8,128)S(1)}, f32[16,8,128]{2,1,0:T(8,128)S(1)}, bf...) custom-call(bf16[128,1024]{1,0:T(8,128)(2,1)} %o.1, ...), custom_call_target="tpu_custom_call" | custom-call | flops 1073741824 | tf_op jit(solution)/shard_map/first_kernel/pallas_call | solution.py:333
  16.2 0.0 copy-start
  16.2 0.0 collective-permute-done.2.d
  16.2 0.5 %collective-permute-done.1.b = bf16[128,1024]{1,0:T(8,128)(2,1)S(1)} collective-permute-done((bf16[128,1024]{1,0:T(8,128)(2,1)}, bf16[128,1024]{1,0:T(8,128)(2,1)S(1)}, u32[]{:S(2)}, u32[]{:S(2)}) %collective-permute-start.1) | collective-permute-done | bytes 262176 | tf_op jit(solution)/shard_map/ppermute | solution.py:330
  16.7 0.3 collective-permute-done.a
  17.0 0.0 collective-permute-start.4
  17.0 0.5 %collective-permute-start.5 = (bf16[128,1024]{1,0:T(8,128)(2,1)S(1)}, bf16[128,1024]{1,0:T(8,128)(2,1)S(1)}, u32[]{:S(2)}, u32[]{:S(2)}) collective-permute-start(bf16[128,1024]{1,0:T(8,128)(2,1)S(1)} %collective-permute-done.1.b), channel_id=1, source_target_pairs={{0,1},{1,0},{2,3},{3,2},{4,5},{5,4},{6,7},{7,6},{8,9},{9,8},{10,11... | collective-permute-start | bytes 786440 | tf_op jit(solution)/shard_map/ppermute | solution.py:326
  17.5 0.0 collective-permute-start.6
  17.5 1.9 %near_kernel.1 = (f32[2,128,1024]{2,1,0:T(8,128)S(1)}, f32[128,128]{1,0:T(8,128)S(1)}) custom-call(bf16[128,1024]{1,0:T(8,128)(2,1)S(1)} %collective-permute-done.a, bf16[128,1024]{1,0:T(8,128)(2,1)S(1)} %collective-permute-done.1.b, bf16[128,1024]{1,0:T(8,128)(2,1)S(1)} %collective-permute-done.2.d, bf16[2,3072,1024]{2,1,0:T(8,128)(2,1)S(1)} %get-tuple-element.31.weights, ...), custom_call_target="tpu_custom_call" | custom-call | flops 1610612736 | tf_op jit(solution)/shard_map/near_kernel/pallas_call | solution.py:333
  19.4 0.0 collective-permute-done.4.a.ao
  19.4 0.0 collective-permute-done.5.b.bo
  19.4 0.0 collective-permute-done.6.d.do
  19.4 0.0 copy-done
  19.4 0.0 copy-start.1
  19.4 4.8 %far_kernel.1 = (f32[128,128]{1,0:T(8,128)S(1)}, f32[128,8,128]{2,1,0:T(8,128)S(1)}, f32[16,8,128]{2,1,0:T(8,128)S(1)}, bf16[1,2048,1024]{2,1,0:T(8,128)(2,1)S(1)}) custom-call(bf16[128,1024]{1,0:T(8,128)(2,1)S(1)} %collective-permute-done.4.a.ao, bf16[128,1024]{1,0:T(8,128)(2,1)S(1)} %collective-permute-done.5.b.bo, ...), custom_call_target="tpu_custom_call" | custom-call | flops 1610612736 | tf_op jit(solution)/shard_map/far_kernel/pallas_call | solution.py:333
  24.2 2.7 %collective-permute-start.8 = (f32[16,8,128]{2,1,0:T(8,128)S(1)}, f32[16,8,128]{2,1,0:T(8,128)S(1)}, u32[]{:S(2)}, u32[]{:S(2)}) collective-permute-start(f32[16,8,128]{2,1,0:T(8,128)S(1)} %get-tuple-element.37), channel_id=1, source_target_pairs={{0,16},{8,24},{16,0},{24,8},{1,17},{9,25},{17,1},{25,9},{2,18},{10... | collective-permute-start | bytes 196616 | tf_op jit(solution)/shard_map/ppermute | solution.py:385
  26.9 1.6 %collective-permute-start.7 = (f32[16,8,128]{2,1,0:T(8,128)S(1)}, f32[16,8,128]{2,1,0:T(8,128)S(1)}, u32[]{:S(2)}, u32[]{:S(2)}) collective-permute-start(f32[16,8,128]{2,1,0:T(8,128)S(1)} %get-tuple-element.37), channel_id=1, source_target_pairs={{0,8},{8,16},{16,24},{24,0},{1,9},{9,17},{17,25},{25,1},{2,10},{10... | collective-permute-start | bytes 196616 | tf_op jit(solution)/shard_map/ppermute | solution.py:385
  28.4 0.0 copy-done.1
  28.4 5.7 %outer_kernel.1 = (f32[128,1024]{1,0:T(8,128)S(1)}, f32[128,8,128]{2,1,0:T(8,128)S(1)}) custom-call(bf16[128,1024]{1,0:T(8,128)(2,1)S(1)} %get-tuple-element.38.o, bf16[128,1024]{1,0:T(8,128)(2,1)S(1)} %collective-permute-done.3.s, bf16[128,1024]{1,0:T(8,128)(2,1)S(1)} %collective-permute-done.a, bf16[128,1024]{1,0:T(8,128)(2,1)S(1)} %collective-permute-done.1.b, ...), custom_call_target="tpu_custom_call" | custom-call | flops 2147483648 | tf_op jit(solution)/shard_map/outer_kernel/pallas_call | solution.py:333
  34.2 0.0 collective-permute-done.8.refs_1_
  34.2 0.0 collective-permute-done.7.refs_0_
  34.2 1.7 %last.1 = bf16[128,1024]{1,0:T(8,128)(2,1)} custom-call(f32[16,8,128]{2,1,0:T(8,128)S(1)} %collective-permute-done.7.refs_0_, f32[16,8,128]{2,1,0:T(8,128)S(1)} %collective-permute-done.8.refs_1_, f32[128,1024]{1,0:T(8,128)S(1)} %get-tuple-element.42.refs_2_, f32[128,8,128]{2,1,0:T(8,128)S(1)} %get-tuple-element.43.refs_3_, ...), custom_call_target="tpu_custom_call" | custom-call | tf_op jit(solution)/shard_map/last/pallas_call | solution.py:399
Async XLA Ops:
  0.0 4.5 %collective-permute-start.3 = (bf16[128,1024]{1,0:T(8,128)(2,1)}, bf16[128,1024]{1,0:T(8,128)(2,1)S(1)}, u32[]{:S(2)}, u32[]{:S(2)}) collective-permute-start(bf16[128,1024]{1,0:T(8,128)(2,1)} %o.1), channel_id=1, source_target_pairs={{0,1},{1,0},{2,3},{3,2},{4,5},{5,4},{6,7},{7,6},{8,9},{9,8},{10,11... | collective-permute-start | bytes 786440 | tf_op jit(solution)/shard_map/ppermute | solution.py:326
  0.5 15.7 %collective-permute-start.2 = (bf16[128,1024]{1,0:T(8,128)(2,1)}, bf16[128,1024]{1,0:T(8,128)(2,1)S(1)}, u32[]{:S(2)}, u32[]{:S(2)}) collective-permute-start(bf16[128,1024]{1,0:T(8,128)(2,1)} %o.1), channel_id=1, source_target_pairs={{0,6},{1,7},{2,4},{3,5},{4,2},{5,3},{6,0},{7,1},{8,14},{9,15},{10,... | collective-permute-start | bytes 786440 | tf_op jit(solution)/shard_map/ppermute | solution.py:326
  3.9 12.8 %collective-permute-start.1 = (bf16[128,1024]{1,0:T(8,128)(2,1)}, bf16[128,1024]{1,0:T(8,128)(2,1)S(1)}, u32[]{:S(2)}, u32[]{:S(2)}) collective-permute-start(bf16[128,1024]{1,0:T(8,128)(2,1)} %o.1), channel_id=1, source_target_pairs={{0,4},{1,3},{2,6},{3,1},{4,0},{5,7},{6,2},{7,5},{8,12},{9,11},{10,... | collective-permute-start | bytes 786440 | tf_op jit(solution)/shard_map/ppermute | solution.py:330
  4.4 12.6 %collective-permute-start = (bf16[128,1024]{1,0:T(8,128)(2,1)}, bf16[128,1024]{1,0:T(8,128)(2,1)S(1)}, u32[]{:S(2)}, u32[]{:S(2)}) collective-permute-start(bf16[128,1024]{1,0:T(8,128)(2,1)} %o.1), channel_id=1, source_target_pairs={{0,2},{1,5},{2,0},{3,7},{4,6},{5,1},{6,4},{7,3},{8,10},{9,13},{10,... | collective-permute-start | bytes 786440 | tf_op jit(solution)/shard_map/ppermute | solution.py:330
  16.2 3.3 %copy-start = (s32[8]{0:T(128)S(1)}, s32[8]{0:T(128)}, u32[]{:S(2)}) copy-start(s32[8]{0:T(128)} %refs_7_.1) | copy-start | bytes 100
  17.0 2.4 %collective-permute-start.4 = (bf16[128,1024]{1,0:T(8,128)(2,1)S(1)}, bf16[128,1024]{1,0:T(8,128)(2,1)S(1)}, u32[]{:S(2)}, u32[]{:S(2)}) collective-permute-start(bf16[128,1024]{1,0:T(8,128)(2,1)S(1)} %collective-permute-done.a), channel_id=1, source_target_pairs={{0,1},{1,0},{2,3},{3,2},{4,5},{5,4},{6,7},{7,6},{8,9},{9,8},{10,11... | collective-permute-start | bytes 786440 | tf_op jit(solution)/shard_map/ppermute | solution.py:326
  17.0 2.4 %collective-permute-start.5 = (bf16[128,1024]{1,0:T(8,128)(2,1)S(1)}, bf16[128,1024]{1,0:T(8,128)(2,1)S(1)}, u32[]{:S(2)}, u32[]{:S(2)}) collective-permute-start(bf16[128,1024]{1,0:T(8,128)(2,1)S(1)} %collective-permute-done.1.b), channel_id=1, source_target_pairs={{0,1},{1,0},{2,3},{3,2},{4,5},{5,4},{6,7},{7,6},{8,9},{9,8},{10,11... | collective-permute-start | bytes 786440 | tf_op jit(solution)/shard_map/ppermute | solution.py:326
  17.5 1.9 %collective-permute-start.6 = (bf16[128,1024]{1,0:T(8,128)(2,1)S(1)}, bf16[128,1024]{1,0:T(8,128)(2,1)S(1)}, u32[]{:S(2)}, u32[]{:S(2)}) collective-permute-start(bf16[128,1024]{1,0:T(8,128)(2,1)S(1)} %collective-permute-done.2.d), channel_id=1, source_target_pairs={{0,1},{1,0},{2,3},{3,2},{4,5},{5,4},{6,7},{7,6},{8,9},{9,8},{10,11... | collective-permute-start | bytes 786440 | tf_op jit(solution)/shard_map/ppermute | solution.py:326
  19.4 9.0 %copy-start.1 = (f32[1024]{0:T(1024)S(1)}, f32[1024]{0:T(1024)}, u32[]{:S(2)}) copy-start(f32[1024]{0:T(1024)} %param.10) | copy-start | bytes 12292
  24.2 10.0 %collective-permute-start.8 = (f32[16,8,128]{2,1,0:T(8,128)S(1)}, f32[16,8,128]{2,1,0:T(8,128)S(1)}, u32[]{:S(2)}, u32[]{:S(2)}) collective-permute-start(f32[16,8,128]{2,1,0:T(8,128)S(1)} %get-tuple-element.37), channel_id=1, source_target_pairs={{0,16},{8,24},{16,0},{24,8},{1,17},{9,25},{17,1},{25,9},{2,18},{10... | collective-permute-start | bytes 196616 | tf_op jit(solution)/shard_map/ppermute | solution.py:385
  26.9 7.3 %collective-permute-start.7 = (f32[16,8,128]{2,1,0:T(8,128)S(1)}, f32[16,8,128]{2,1,0:T(8,128)S(1)}, u32[]{:S(2)}, u32[]{:S(2)}) collective-permute-start(f32[16,8,128]{2,1,0:T(8,128)S(1)} %get-tuple-element.37), channel_id=1, source_target_pairs={{0,8},{8,16},{16,24},{24,0},{1,9},{9,17},{17,25},{25,1},{2,10},{10... | collective-permute-start | bytes 196616 | tf_op jit(solution)/shard_map/ppermute | solution.py:385

commit v2 on v1

--- a/solution.py
+++ b/solution.py
@@ -11,7 +11,6 @@
 LANE = 128
 IN_VMEM = pl.BlockSpec(memory_space=pltpu.VMEM)
 IN_HBM = pl.BlockSpec(memory_space=pltpu.HBM)
-IN_SMEM = pl.BlockSpec(memory_space=pltpu.SMEM)
 DRIVEN = (1, 2)
 GATE = (0,)
 
@@ -140,19 +139,21 @@
 
 
 def first_kernel(
-    o, s, wt, rate, res, acc, sq, lam3, mix3, held, near, far, wbuf, rates, ress, sem, small
+    o, s, wt, rate, res, lengths, acc, outer, sq, lam3, mix3, near, far, gate, rowmask, valid, held, wbuf, gbuf, rates, ress, docs, sem, small
 ):
-    depth = s.shape[1]
+    rows, depth = s.shape
     own = [
         pltpu.make_async_copy(o, held, small.at[0]),
         pltpu.make_async_copy(rate, rates, small.at[1]),
         pltpu.make_async_copy(res, ress, small.at[2]),
+        pltpu.make_async_copy(lengths, docs, small.at[3]),
     ]
-    for c in own:
-        c.start()
     copies = weight_copies(wt, DRIVEN, (0, 1), depth, wbuf, sem)
-    copies += weight_copies(wt, DRIVEN, own_masks(), depth, near, sem, 4)
-    copies += weight_copies(wt, DRIVEN, other_masks(), depth, far, sem, 10)
+    copies += weight_copies(wt, GATE, (0, 1), depth, gbuf, sem, 4)
+    copies += weight_copies(wt, DRIVEN, own_masks(), depth, near, sem, 6)
+    copies += weight_copies(wt, DRIVEN, other_masks()[:2], depth, far, sem, 12)
+    copies += weight_copies(wt, GATE, own_masks()[:1], depth, gate, sem, 16)
+    run_copies(own, len(own))
     wait = run_copies(copies, 8)
     for c in own:
         c.wait()
@@ -171,56 +172,69 @@
 
     by_groups(lam, put_lam)
     by_groups(mix, put_mix)
+    mark_rows(docs, rows, rowmask, valid)
     for k in range(2):
         wait(2 * k)
         wait(2 * k + 1)
         acc[k] = project(blocks, wbuf, k)
-    for i in range(4, len(copies)):
+    wait(4)
+    wait(5)
+    outer[...] = project(blocks, gbuf, 0)
+    for i in range(6, len(copies)):
         wait(i)
 
 
-def near_kernel(a, b, d, weights, acc_in, sq_in, acc, sq):
+def near_kernel(a, b, d, weights, wt, acc_in, sq_in, acc, sq, far, sem):
     blocks = (a, b, d)
+    wait = run_copies(weight_copies(wt, DRIVEN, other_masks()[2:], a.shape[1], far, sem), 8)
     sq[...] = add_squares(sq_in[...], blocks)
-    for k in range(2):
+
+    @pl.loop(0, 2)
+    def _(k):
         acc[k] = acc_in[k] + project(blocks, weights, k)
 
-
-def far_kernel(a, b, d, weights, wt, acc_in, sq_in, lam3, docs, scale, d3, e3, gate, sem):
+    for i in range(2):
+        wait(i)
+
+
+def far_kernel(
+    a, b, d, weights, last_weights, wt, acc_in, sq_in, lam3, rowmask, scale, d3, e3, gate, both, sem
+):
     rows, depth = a.shape
-    wait = run_copies(weight_copies(wt, GATE, (0, 1), depth, gate, sem), 8)
+    wait = run_copies(weight_copies(wt, GATE, own_masks()[1:] + other_masks()[:1], depth, gate, sem), 8)
     blocks = (a, b, d)
     total = jnp.sum(add_squares(sq_in[...], blocks), axis=1, keepdims=True)
     row = lax.rsqrt(total / (8 * depth) + 1e-06)
     scale[...] = jnp.broadcast_to(row, scale.shape)
-    inner = acc_in[0] + project(blocks, weights, 0)
-    values = acc_in[1] + project(blocks, weights, 1)
-    driven = (inner * row) * (values * row)
-
-    def put(g, v):
-        d3[:, g, :] = v
-
-    by_groups(driven, put)
-    _, last, _ = own_starts(docs, rows)
+
+    @pl.loop(0, 2)
+    def _(k):
+        both[k] = acc_in[k] + project((a, b), weights, k) + project((d,), last_weights, k)
+
+    for g in range(SUB):
+        cols = slice(g * LANE, (g + 1) * LANE)
+        d3[:, g, :] = (both[0, :, cols] * scale[...]) * (both[1, :, cols] * scale[...])
     modes = lam3.shape[0]
 
     def body(step, state):
+        first = pl.multiple_of(step * SUB, SUB)
+        counts = rowmask[0, pl.ds(first, SUB), :]
         for j in range(SUB):
-            t = step * SUB + j
-            drive = jnp.where(t >= last, d3[t], 0.0)
+            drive = d3[first + j] * counts[j : j + 1, :]
             state = [lam3[n] * state[n] + drive for n in range(modes)]
         return state
 
     zeros = [jnp.zeros((SUB, LANE), jnp.float32) for _ in range(modes)]
-    state = lax.fori_loop(jnp.maximum(last, 0) // SUB, rows // SUB, body, zeros)
+    state = lax.fori_loop(0, rows // SUB, body, zeros)
     for n in range(modes):
         e3[n] = state[n]
-    for i in range(2):
+    for i in range(3):
         wait(i)
 
 
-def own_starts(docs, rows):
-    at = -lax.axis_index("ctx") * rows
+def mark_rows(docs, rows, rowmask, valid):
+    me = lax.axis_index("ctx")
+    at = -me * rows
     first, last, starts = rows, -1, []
     for i in range(docs.shape[0]):
         inside = jnp.logical_and(at >= 0, at < rows)
@@ -228,81 +242,84 @@
         last = jnp.where(jnp.logical_and(inside, at > last), at, last)
         starts.append(at)
         at = at + docs[i]
-    return first, last, starts
+    token = lax.broadcasted_iota(jnp.int32, rowmask.shape[1:], 0)
+    rowmask[0] = jnp.where(token >= last, 1.0, 0.0)
+    keep = jnp.ones(rowmask.shape[1:], jnp.float32)
+    for at in starts:
+        keep = jnp.where(token == at, 0.0, keep)
+    rowmask[1] = keep
+    rowmask[2] = jnp.where(token < first, 1.0, 0.0)
+    reached = me >= 1
+    for k in range(valid.shape[0]):
+        if k > 0:
+            for at in starts:
+                between = jnp.logical_and(at >= -k * rows, at < -(k - 1) * rows)
+                reached = jnp.logical_and(reached, jnp.logical_not(between))
+            reached = jnp.logical_and(reached, me >= k + 1)
+        valid[k] = jnp.full(valid.shape[1:], jnp.where(reached, 1.0, 0.0))
 
 
 def outer_kernel(
-    o, s, a, b, d, ao, bo, do, wt, gate, d3, lam3, mix3, skip, docs, outer, f3, wbuf, sem
+    a, b, d, ao, bo, do, wt, sum_in, gate_a, gate_far, d3, lam3, mix3, skip, rowmask, outer, f3, wbuf, sem
 ):
-    rows, depth = o.shape
-    masks = own_masks() + other_masks()
-    wait = run_copies(weight_copies(wt, GATE, masks, depth, wbuf, sem), 8)
+    rows, depth = a.shape
     modes = lam3.shape[0]
-    _, _, starts = own_starts(docs, rows)
+    wait = run_copies(weight_copies(wt, GATE, other_masks()[1:], depth, wbuf, sem), 8)
 
     def body(step, state):
+        first = pl.multiple_of(step * SUB, SUB)
+        keeps = rowmask[1, pl.ds(first, SUB), :]
         for j in range(SUB):
-            t = step * SUB + j
-            begins = starts[0] == t
-            for at in starts[1:]:
-                begins = jnp.logical_or(begins, at == t)
-            keep = jnp.where(begins, 0.0, 1.0)
-            drive = d3[t]
-            state = [lam3[n] * (state[n] * keep) + drive for n in range(modes)]
+            drive = d3[first + j]
+            state = [lam3[n] * (state[n] * keeps[j : j + 1, :]) + drive for n in range(modes)]
             terms = [mix3[n] * state[n] for n in range(modes)]
             while len(terms) > 1:
                 terms = [p + q for p, q in zip(terms[::2], terms[1::2])]
-            f3[t] = terms[0] + skip[...] * drive
+            f3[first + j] = terms[0] + skip[...] * drive
         return state
 
     zeros = [jnp.zeros((SUB, LANE), jnp.float32) for _ in range(modes)]
     lax.fori_loop(0, rows // SUB, body, zeros)
-    total = project((o, s), gate, 0)
-    for i, block in enumerate((a, b, d, ao, bo, do)):
-        wait(i)
-        total = total + dot(block[...], wbuf[0, i * depth : (i + 1) * depth])
-    outer[...] = total
+    total = sum_in[...] + project((a,), gate_a, 0) + project((b, d, ao), gate_far, 0)
+    wait(0)
+    wait(1)
+    outer[...] = total + project((bo, do), wbuf, 0)
 
 
 def last_kernel(*refs, count):
     arrived = refs[:count]
-    outer, f3, scale, lam3, mix3, docs, out = refs[count:]
+    outer, f3, scale, lam3, mix3, rowmask, valid, out = refs[count:]
     rows = outer.shape[0]
     modes = lam3.shape[0]
-    first, _, starts = own_starts(docs, rows)
-    me = lax.axis_index("ctx")
-    begins, valid = [], None
-    for k in range(1, count + 1):
-        if k > 1:
-            inside = [jnp.logical_and(at >= -(k - 1) * rows, at < -(k - 2) * rows) for at in starts]
-            clear = jnp.logical_not(functools.reduce(jnp.logical_or, inside))
-            valid = jnp.logical_and(jnp.logical_and(valid, clear), me >= k)
-        else:
-            valid = me >= 1
-        begins.append(valid)
-    state = []
-    for n in range(modes):
-        lam = lam3[n]
-        whole = lam
-        for _ in range(rows.bit_length() - 1):
-            whole = whole * whole
-        power, total = 1.0, jnp.zeros((SUB, LANE), jnp.float32)
-        for k in range(count):
-            total = total + jnp.where(begins[k], power * arrived[k][n], 0.0)
-            power = power * whole
-        state.append(mix3[n] * total)
-
-    def body(step, state):
-        for j in range(SUB):
-            t = step * SUB + j
-            state = [lam3[n] * state[n] for n in range(modes)]
-            terms = list(state)
-            while len(terms) > 1:
-                terms = [a + b for a, b in zip(terms[::2], terms[1::2])]
-            f3[t] = f3[t] + jnp.where(t < first, terms[0], 0.0)
-        return state
-
-    lax.fori_loop(0, (first + SUB - 1) // SUB, body, state)
+    @pl.when(lax.axis_index("ctx") > 0)
+    def _():
+        state = []
+        for n in range(modes):
+            lam = lam3[n]
+            whole = lam
+            for _ in range(rows.bit_length() - 1):
+                whole = whole * whole
+            power, total = valid[0], jnp.zeros((SUB, LANE), jnp.float32)
+            for k in range(count):
+                total = total + power * arrived[k][n]
+                if k + 1 < count:
+                    power = valid[k + 1] * whole if k == 0 else valid[k + 1] * (power * whole)
+            state.append(mix3[n] * total)
+
+        def body(step, state):
+            first = pl.multiple_of(step * SUB, SUB)
+            reached = rowmask[2, pl.ds(first, SUB), :]
+            for j in range(SUB):
+                t = first + j
+                state = [lam3[n] * state[n] for n in range(modes)]
+                terms = list(state)
+                while len(terms) > 1:
+                    terms = [a + b for a, b in zip(terms[::2], terms[1::2])]
+                f3[t] = f3[t] + terms[0] * reached[j : j + 1, :]
+            return state
+
+        lax.fori_loop(0, rows // SUB, body, state)
+
     for g in range(SUB):
         cols = slice(g * LANE, (g + 1) * LANE)
         out[:, cols] = (outer[:, cols] * scale[...] * f3[:, g, :]).astype(out.dtype)
@@ -347,6 +364,7 @@
         return [(IN_VMEM, a) for a in arrays]
 
     planes = pltpu.VMEM((2, rows, local), f32)
+    product = pltpu.VMEM((rows, local), f32)
     squares = pltpu.VMEM((rows, LANE), f32)
     poles = pltpu.VMEM((modes, SUB, LANE), f32)
     tokens = pltpu.VMEM((rows, SUB, LANE), f32)
@@ -361,22 +379,30 @@
 
     s = swap(stream, 1)
     a, b, d = split(stream, True), split(stream, False), swap(stream, 6)
-    acc, sq, lam3, mix3, o, near, far = call(
+    acc, outer, sq, lam3, mix3, near, far, gate_a, rowmask, valid = call(
         first_kernel,
-        there(stream) + here(s) + there(wt, rate, res),
-        [planes, squares, poles, poles, chunk, weights(2, 3), weights(2, 3)],
-        [weights(2, 2), vector, vector, dma((16,)), dma((3,))],
+        there(stream) + here(s) + there(wt, rate, res, doc_lengths),
+        [planes, product, squares, poles, poles, weights(2, 3), weights(2, 2), weights(1, 1)]
+        + [pltpu.VMEM((3, rows, LANE), f32), pltpu.VMEM((reach, SUB, LANE), f32)],
+        [chunk, weights(2, 2), weights(1, 2), vector, vector, pltpu.SMEM(doc_lengths.shape, jnp.int32), dma((17,)), dma((4,))],
         4,
-        12,
+        16,
     )
     a, b, d, acc, sq = lax.optimization_barrier((a, b, d, acc, sq))
     ao, bo, do = swap(a, 1), swap(b, 1), swap(d, 1)
-    acc, sq = call(near_kernel, here(a, b, d, near, acc, sq), [planes, squares], [], 6, 4)
-    scale, d3, e3, gate = call(
+    acc, sq, far_d = call(
+        near_kernel,
+        here(a, b, d, near) + there(wt) + here(acc, sq),
+        [planes, squares, weights(2, 1)],
+        [dma((2,))],
+        6,
+        4,
+    )
+    scale, d3, e3, gate_far = call(
         far_kernel,
-        here(ao, bo, do, far) + there(wt) + here(acc, sq, lam3) + [(IN_SMEM, doc_lengths)],
-        [squares, tokens, poles, weights(1, 2)],
-        [dma((2,))],
+        here(ao, bo, do, far, far_d) + there(wt) + here(acc, sq, lam3, rowmask),
+        [squares, tokens, poles, weights(1, 3)],
+        [planes, dma((3,))],
         6,
         4,
     )
@@ -387,23 +413,22 @@
     ]
     outer, f3 = call(
         outer_kernel,
-        here(o, s, a, b, d, ao, bo, do)
+        here(a, b, d, ao, bo, do)
         + there(wt)
-        + here(gate, d3, lam3, mix3, skip_gain.reshape(SUB, LANE))
-        + [(IN_SMEM, doc_lengths)],
-        [pltpu.VMEM((rows, local), f32), tokens],
-        [weights(1, 6), dma((6,))],
+        + here(outer, gate_a, gate_far, d3, lam3, mix3, skip_gain.reshape(SUB, LANE), rowmask),
+        [product, tokens],
+        [weights(1, 2), dma((2,))],
         8,
         16,
     )
     return pl.pallas_call(
         functools.partial(last_kernel, count=reach),
-        in_specs=[IN_VMEM] * (reach + 5) + [IN_SMEM],
+        in_specs=[IN_VMEM] * (reach + 7),
         out_specs=IN_VMEM,
         out_shape=jax.ShapeDtypeStruct((rows, local), b16),
         compiler_params=params(8),
         name="last",
-    )(*arrived, outer, f3, scale, lam3, mix3, doc_lengths)
+    )(*arrived, outer, f3, scale, lam3, mix3, rowmask, valid)
 
 
 def solution(mesh):

time: 36 us -> 33 us (0.917)
  Pallas kernels: 25.6 us -> 21.7 us
  waiting for transfers between devices: 0.83 us -> 1.74 us
    pallas_call x4, Pallas kernels: 24 us -> 20.7 us  [call(): pl.pallas_call(kernel, in_specs=[spec for spec, _ in ins], out_specs=[IN_...]
    ppermute x2, waiting for transfers between devices: 0.01 us -> 1.06 us  [fitted(): lax.ppermute(e3, 'ctx', [(i, (i + k) % ring) for i in range(ring)])]
    pallas_call x1, Pallas kernels: 1.65 us -> 1.05 us  [fitted(): pl.pallas_call(functools.partial(last_kernel, count=reach), in_specs=[IN_...]
  transfers between devices with their start and end apart: 9 -> 9, of which waited for: 2 -> 3; matrix products, arithmetic and copies ran while one was open for 0% -> 0% of each run, Pallas kernels for 54% -> 53%
where the time goes in v2:
time: 33 us; the launch traced here: 32.8 us
  Pallas kernels  21.7 us (66%)
  starting transfers between devices  9.29 us (28%)
  waiting for transfers between devices  1.74 us (5%)
    pallas_call x4, Pallas kernels, call(): pl.pallas_call(kernel, in_specs=[spec for spec, _ in ins], out_specs=[IN_...  20.7 us
    ppermute x5, starting transfers between devices, swap(): return lax.ppermute(block, 'ch', [(i, i ^ mask) for i in range(size)])  4.41 us
    ppermute x2, starting transfers between devices, fitted(): lax.ppermute(e3, 'ctx', [(i, (i + k) % ring) for i in range(ring)])  4.24 us
    ppermute x2, waiting for transfers between devices, fitted(): lax.ppermute(e3, 'ctx', [(i, (i + k) % ring) for i in range(ring)])  1.06 us
    pallas_call x1, Pallas kernels, fitted(): pl.pallas_call(functools.partial(last_kernel, count=reach), in_specs=[IN_...  1.05 us
    ppermute x2, waiting for transfers between devices, split(): lax.ppermute(block, 'ch', [(i, i ^ masks[i & 1]) for i in range(size)])  0.66 us
  transfers between devices with their start and end apart: 9, of which 3 were waited for; matrix products, arithmetic and copies ran while one was open for 0% of the time, Pallas kernels for 53%

profile of v2, /device:TPU:0, one launch (start us, length us, event | category | flops | bytes accessed | tf_op | source)
XLA Modules:
  0.0 32.8 jit_solution(12564576577527361513)
XLA Ops:
  0.0 0.5 %collective-permute-start.3 = (bf16[128,1024]{1,0:T(8,128)(2,1)}, bf16[128,1024]{1,0:T(8,128)(2,1)S(1)}, u32[]{:S(2)}, u32[]{:S(2)}) collective-permute-start(bf16[128,1024]{1,0:T(8,128)(2,1)} %o.1), channel_id=1, source_target_pairs={{0,1},{1,0},{2,3},{3,2},{4,5},{5,4},{6,7},{7,6},{8,9},{9,8},{10,11... | collective-permute-start | bytes 786440 | tf_op jit(solution)/shard_map/ppermute | solution.py:343
  0.5 3.4 %collective-permute-start.2 = (bf16[128,1024]{1,0:T(8,128)(2,1)}, bf16[128,1024]{1,0:T(8,128)(2,1)S(1)}, u32[]{:S(2)}, u32[]{:S(2)}) collective-permute-start(bf16[128,1024]{1,0:T(8,128)(2,1)} %o.1), channel_id=1, source_target_pairs={{0,6},{1,7},{2,4},{3,5},{4,2},{5,3},{6,0},{7,1},{8,14},{9,15},{10,... | collective-permute-start | bytes 786440 | tf_op jit(solution)/shard_map/ppermute | solution.py:343
  3.9 0.5 %collective-permute-start.1 = (bf16[128,1024]{1,0:T(8,128)(2,1)}, bf16[128,1024]{1,0:T(8,128)(2,1)S(1)}, u32[]{:S(2)}, u32[]{:S(2)}) collective-permute-start(bf16[128,1024]{1,0:T(8,128)(2,1)} %o.1), channel_id=1, source_target_pairs={{0,4},{1,3},{2,6},{3,1},{4,0},{5,7},{6,2},{7,5},{8,12},{9,11},{10,... | collective-permute-start | bytes 786440 | tf_op jit(solution)/shard_map/ppermute | solution.py:347
  4.4 0.1 collective-permute-start
  4.5 0.0 collective-permute-done.3.s
  4.5 11.8 %first_kernel.1 = (f32[2,128,1024]{2,1,0:T(8,128)S(1)}, f32[128,1024]{1,0:T(8,128)S(1)}, f32[128,128]{1,0:T(8,128)S(1)}, f32[16,8,128]{2,1,0:T(8,128)S(1)}, f32[...) custom-call(bf16[128,1024]{1,0:T(8,128)(2,1)} %o.1, ...), custom_call_target="tpu_custom_call" | custom-call | flops 1073741824 | tf_op jit(solution)/shard_map/first_kernel/pallas_call | solution.py:350
  16.3 0.0 collective-permute-done.2.d
  16.3 0.4 %collective-permute-done.1.b = bf16[128,1024]{1,0:T(8,128)(2,1)S(1)} collective-permute-done((bf16[128,1024]{1,0:T(8,128)(2,1)}, bf16[128,1024]{1,0:T(8,128)(2,1)S(1)}, u32[]{:S(2)}, u32[]{:S(2)}) %collective-permute-start.1) | collective-permute-done | bytes 262176 | tf_op jit(solution)/shard_map/ppermute | solution.py:347
  16.7 0.3 collective-permute-done.a
  17.0 0.0 collective-permute-start.4
  17.0 0.5 %collective-permute-start.5 = (bf16[128,1024]{1,0:T(8,128)(2,1)S(1)}, bf16[128,1024]{1,0:T(8,128)(2,1)S(1)}, u32[]{:S(2)}, u32[]{:S(2)}) collective-permute-start(bf16[128,1024]{1,0:T(8,128)(2,1)S(1)} %collective-permute-done.1.b), channel_id=1, source_target_pairs={{0,1},{1,0},{2,3},{3,2},{4,5},{5,4},{6,7},{7,6},{8,9},{9,8},{10,11... | collective-permute-start | bytes 786440 | tf_op jit(solution)/shard_map/ppermute | solution.py:343
  17.5 0.0 collective-permute-start.6
  17.5 2.2 %near_kernel.1 = (f32[2,128,1024]{2,1,0:T(8,128)S(1)}, f32[128,128]{1,0:T(8,128)S(1)}, bf16[2,1024,1024]{2,1,0:T(8,128)(2,1)S(1)}) custom-call(bf16[128,1024]{1,0:T(8,128)(2,1)S(1)} %collective-permute-done.a, bf16[128,1024]{1,0:T(8,128)(2,1)S(1)} %collective-permute-done.1.b, bf16[128,1024]{1,0:T(8,128)(2,1)S(1)} %collective-permute-done.2.d, ...), custom_call_target="tpu_custom_call" | custom-call | flops 1610612736 | tf_op jit(solution)/shard_map/near_kernel/pallas_call | solution.py:350
  19.8 0.0 collective-permute-done.4.a.ao
  19.8 0.0 collective-permute-done.5.b.bo
  19.8 0.0 collective-permute-done.6.d.do
  19.8 0.0 copy-start
  19.8 3.2 %far_kernel.1 = (f32[128,128]{1,0:T(8,128)S(1)}, f32[128,8,128]{2,1,0:T(8,128)S(1)}, f32[16,8,128]{2,1,0:T(8,128)S(1)}, bf16[1,3072,1024]{2,1,0:T(8,128)(2,1)S(1)}) custom-call(bf16[128,1024]{1,0:T(8,128)(2,1)S(1)} %collective-permute-done.4.a.ao, bf16[128,1024]{1,0:T(8,128)(2,1)S(1)} %collective-permute-done.5.b.bo, ...), custom_call_target="tpu_custom_call" | custom-call | flops 1610612736 | tf_op jit(solution)/shard_map/far_kernel/pallas_call | solution.py:350
  23.1 2.7 %collective-permute-start.8 = (f32[16,8,128]{2,1,0:T(8,128)S(1)}, f32[16,8,128]{2,1,0:T(8,128)S(1)}, u32[]{:S(2)}, u32[]{:S(2)}) collective-permute-start(f32[16,8,128]{2,1,0:T(8,128)S(1)} %get-tuple-element.43), channel_id=1, source_target_pairs={{0,16},{8,24},{16,0},{24,8},{1,17},{9,25},{17,1},{25,9},{2,18},{10... | collective-permute-start | bytes 196616 | tf_op jit(solution)/shard_map/ppermute | solution.py:411
  25.7 1.6 %collective-permute-start.7 = (f32[16,8,128]{2,1,0:T(8,128)S(1)}, f32[16,8,128]{2,1,0:T(8,128)S(1)}, u32[]{:S(2)}, u32[]{:S(2)}) collective-permute-start(f32[16,8,128]{2,1,0:T(8,128)S(1)} %get-tuple-element.43), channel_id=1, source_target_pairs={{0,8},{8,16},{16,24},{24,0},{1,9},{9,17},{17,25},{25,1},{2,10},{10... | collective-permute-start | bytes 196616 | tf_op jit(solution)/shard_map/ppermute | solution.py:411
  27.3 0.0 copy-done
  27.3 3.4 %outer_kernel.1 = (f32[128,1024]{1,0:T(8,128)S(1)}, f32[128,8,128]{2,1,0:T(8,128)S(1)}) custom-call(bf16[128,1024]{1,0:T(8,128)(2,1)S(1)} %collective-permute-done.a, bf16[128,1024]{1,0:T(8,128)(2,1)S(1)} %collective-permute-done.1.b, bf16[128,1024]{1,0:T(8,128)(2,1)S(1)} %collective-permute-done.2.d, bf16[128,1024]{1,0:T(8,128)(2,1)S(1)} %collective-permute-done.4.a.ao, ...), custom_call_target="tpu_custom_call" | custom-call | flops 2147483648 | tf_op jit(solution)/shard_map/outer_kernel/pallas_call | solution.py:350
  30.7 0.0 collective-permute-done.8.refs_1_
  30.7 1.1 %collective-permute-done.7.refs_0_ = f32[16,8,128]{2,1,0:T(8,128)S(1)} collective-permute-done((f32[16,8,128]{2,1,0:T(8,128)S(1)}, f32[16,8,128]{2,1,0:T(8,128)S(1)}, u32[]{:S(2)}, u32[]{:S(2)}) %collective-permute-start.7) | collective-permute-done | bytes 65568 | tf_op jit(solution)/shard_map/ppermute | solution.py:411
  31.8 1.0 %last.1 = bf16[128,1024]{1,0:T(8,128)(2,1)} custom-call(f32[16,8,128]{2,1,0:T(8,128)S(1)} %collective-permute-done.7.refs_0_, f32[16,8,128]{2,1,0:T(8,128)S(1)} %collective-permute-done.8.refs_1_, f32[128,1024]{1,0:T(8,128)S(1)} %get-tuple-element.49.refs_2_, f32[128,8,128]{2,1,0:T(8,128)S(1)} %get-tuple-element.50.refs_3_, ...), custom_call_target="tpu_custom_call" | custom-call | tf_op jit(solution)/shard_map/last/pallas_call | solution.py:424
Async XLA Ops:
  0.0 4.5 %collective-permute-start.3 = (bf16[128,1024]{1,0:T(8,128)(2,1)}, bf16[128,1024]{1,0:T(8,128)(2,1)S(1)}, u32[]{:S(2)}, u32[]{:S(2)}) collective-permute-start(bf16[128,1024]{1,0:T(8,128)(2,1)} %o.1), channel_id=1, source_target_pairs={{0,1},{1,0},{2,3},{3,2},{4,5},{5,4},{6,7},{7,6},{8,9},{9,8},{10,11... | collective-permute-start | bytes 786440 | tf_op jit(solution)/shard_map/ppermute | solution.py:343
  0.5 15.9 %collective-permute-start.2 = (bf16[128,1024]{1,0:T(8,128)(2,1)}, bf16[128,1024]{1,0:T(8,128)(2,1)S(1)}, u32[]{:S(2)}, u32[]{:S(2)}) collective-permute-start(bf16[128,1024]{1,0:T(8,128)(2,1)} %o.1), channel_id=1, source_target_pairs={{0,6},{1,7},{2,4},{3,5},{4,2},{5,3},{6,0},{7,1},{8,14},{9,15},{10,... | collective-permute-start | bytes 786440 | tf_op jit(solution)/shard_map/ppermute | solution.py:343
  3.9 12.8 %collective-permute-start.1 = (bf16[128,1024]{1,0:T(8,128)(2,1)}, bf16[128,1024]{1,0:T(8,128)(2,1)S(1)}, u32[]{:S(2)}, u32[]{:S(2)}) collective-permute-start(bf16[128,1024]{1,0:T(8,128)(2,1)} %o.1), channel_id=1, source_target_pairs={{0,4},{1,3},{2,6},{3,1},{4,0},{5,7},{6,2},{7,5},{8,12},{9,11},{10,... | collective-permute-start | bytes 786440 | tf_op jit(solution)/shard_map/ppermute | solution.py:347
  4.4 12.6 %collective-permute-start = (bf16[128,1024]{1,0:T(8,128)(2,1)}, bf16[128,1024]{1,0:T(8,128)(2,1)S(1)}, u32[]{:S(2)}, u32[]{:S(2)}) collective-permute-start(bf16[128,1024]{1,0:T(8,128)(2,1)} %o.1), channel_id=1, source_target_pairs={{0,2},{1,5},{2,0},{3,7},{4,6},{5,1},{6,4},{7,3},{8,10},{9,13},{10,... | collective-permute-start | bytes 786440 | tf_op jit(solution)/shard_map/ppermute | solution.py:347
  17.0 2.8 %collective-permute-start.4 = (bf16[128,1024]{1,0:T(8,128)(2,1)S(1)}, bf16[128,1024]{1,0:T(8,128)(2,1)S(1)}, u32[]{:S(2)}, u32[]{:S(2)}) collective-permute-start(bf16[128,1024]{1,0:T(8,128)(2,1)S(1)} %collective-permute-done.a), channel_id=1, source_target_pairs={{0,1},{1,0},{2,3},{3,2},{4,5},{5,4},{6,7},{7,6},{8,9},{9,8},{10,11... | collective-permute-start | bytes 786440 | tf_op jit(solution)/shard_map/ppermute | solution.py:343
  17.0 2.8 %collective-permute-start.5 = (bf16[128,1024]{1,0:T(8,128)(2,1)S(1)}, bf16[128,1024]{1,0:T(8,128)(2,1)S(1)}, u32[]{:S(2)}, u32[]{:S(2)}) collective-permute-start(bf16[128,1024]{1,0:T(8,128)(2,1)S(1)} %collective-permute-done.1.b), channel_id=1, source_target_pairs={{0,1},{1,0},{2,3},{3,2},{4,5},{5,4},{6,7},{7,6},{8,9},{9,8},{10,11... | collective-permute-start | bytes 786440 | tf_op jit(solution)/shard_map/ppermute | solution.py:343
  17.5 2.3 %collective-permute-start.6 = (bf16[128,1024]{1,0:T(8,128)(2,1)S(1)}, bf16[128,1024]{1,0:T(8,128)(2,1)S(1)}, u32[]{:S(2)}, u32[]{:S(2)}) collective-permute-start(bf16[128,1024]{1,0:T(8,128)(2,1)S(1)} %collective-permute-done.2.d), channel_id=1, source_target_pairs={{0,1},{1,0},{2,3},{3,2},{4,5},{5,4},{6,7},{7,6},{8,9},{9,8},{10,11... | collective-permute-start | bytes 786440 | tf_op jit(solution)/shard_map/ppermute | solution.py:343
  19.8 7.5 %copy-start = (f32[1024]{0:T(1024)S(1)}, f32[1024]{0:T(1024)}, u32[]{:S(2)}) copy-start(f32[1024]{0:T(1024)} %param.10) | copy-start | bytes 12292
  23.1 7.7 %collective-permute-start.8 = (f32[16,8,128]{2,1,0:T(8,128)S(1)}, f32[16,8,128]{2,1,0:T(8,128)S(1)}, u32[]{:S(2)}, u32[]{:S(2)}) collective-permute-start(f32[16,8,128]{2,1,0:T(8,128)S(1)} %get-tuple-element.43), channel_id=1, source_target_pairs={{0,16},{8,24},{16,0},{24,8},{1,17},{9,25},{17,1},{25,9},{2,18},{10... | collective-permute-start | bytes 196616 | tf_op jit(solution)/shard_map/ppermute | solution.py:411
  25.7 6.1 %collective-permute-start.7 = (f32[16,8,128]{2,1,0:T(8,128)S(1)}, f32[16,8,128]{2,1,0:T(8,128)S(1)}, u32[]{:S(2)}, u32[]{:S(2)}) collective-permute-start(f32[16,8,128]{2,1,0:T(8,128)S(1)} %get-tuple-element.43), channel_id=1, source_target_pairs={{0,8},{8,16},{16,24},{24,0},{1,9},{9,17},{17,25},{25,1},{2,10},{10... | collective-permute-start | bytes 196616 | tf_op jit(solution)/shard_map/ppermute | solution.py:411

commit v3 on v2

--- a/solution.py
+++ b/solution.py
@@ -301,7 +301,7 @@
                 whole = whole * whole
             power, total = valid[0], jnp.zeros((SUB, LANE), jnp.float32)
             for k in range(count):
-                total = total + power * arrived[k][n]
+                total = total + power * arrived[k][n].astype(jnp.float32)
                 if k + 1 < count:
                     power = valid[k + 1] * whole if k == 0 else valid[k + 1] * (power * whole)
             state.append(mix3[n] * total)
@@ -408,7 +408,7 @@
     )
     ring = lax.axis_size("ctx")
     arrived = [
-        lax.ppermute(e3, "ctx", [(i, (i + k) % ring) for i in range(ring)])
+        lax.ppermute(e3 if k == 1 else e3.astype(b16), "ctx", [(i, (i + k) % ring) for i in range(ring)])
         for k in range(1, reach + 1)
     ]
     outer, f3 = call(

time: 33 us -> 32.1 us (0.973)
  waiting for transfers between devices: 1.74 us -> 0.86 us
    ppermute x2, waiting for transfers between devices: 1.06 us -> 0.18 us  [fitted(): lax.ppermute(e3 if k == 1 else e3.astype(b16), 'ctx', [(i, (i + k) % ring...]
  transfers between devices with their start and end apart: 9 -> 9, of which waited for: 3 -> 3; matrix products, arithmetic and copies ran while one was open for 0% -> 0% of each run, Pallas kernels for 53% -> 54%
where the time goes in v3:
time: 32.1 us; the launch traced here: 32 us
  Pallas kernels  21.7 us (68%)
  starting transfers between devices  9.27 us (29%)
  waiting for transfers between devices  0.86 us (3%)
    pallas_call x4, Pallas kernels, call(): pl.pallas_call(kernel, in_specs=[spec for spec, _ in ins], out_specs=[IN_...  20.7 us
    ppermute x5, starting transfers between devices, swap(): return lax.ppermute(block, 'ch', [(i, i ^ mask) for i in range(size)])  4.41 us
    ppermute x2, starting transfers between devices, fitted(): lax.ppermute(e3 if k == 1 else e3.astype(b16), 'ctx', [(i, (i + k) % ring...  4.23 us
    pallas_call x1, Pallas kernels, fitted(): pl.pallas_call(functools.partial(last_kernel, count=reach), in_specs=[IN_...  1.05 us
    ppermute x2, waiting for transfers between devices, split(): lax.ppermute(block, 'ch', [(i, i ^ masks[i & 1]) for i in range(size)])  0.66 us
  transfers between devices with their start and end apart: 9, of which 3 were waited for; matrix products, arithmetic and copies ran while one was open for 0% of the time, Pallas kernels for 54%

profile of v3, /device:TPU:0, one launch (start us, length us, event | category | flops | bytes accessed | tf_op | source)
XLA Modules:
  0.0 32.0 jit_solution(13064375783857494417)
XLA Ops:
  0.0 0.5 %collective-permute-start.3 = (bf16[128,1024]{1,0:T(8,128)(2,1)}, bf16[128,1024]{1,0:T(8,128)(2,1)S(1)}, u32[]{:S(2)}, u32[]{:S(2)}) collective-permute-start(bf16[128,1024]{1,0:T(8,128)(2,1)} %o.1), channel_id=1, source_target_pairs={{0,1},{1,0},{2,3},{3,2},{4,5},{5,4},{6,7},{7,6},{8,9},{9,8},{10,11... | collective-permute-start | bytes 786440 | tf_op jit(solution)/shard_map/ppermute | solution.py:343
  0.5 3.4 %collective-permute-start.2 = (bf16[128,1024]{1,0:T(8,128)(2,1)}, bf16[128,1024]{1,0:T(8,128)(2,1)S(1)}, u32[]{:S(2)}, u32[]{:S(2)}) collective-permute-start(bf16[128,1024]{1,0:T(8,128)(2,1)} %o.1), channel_id=1, source_target_pairs={{0,6},{1,7},{2,4},{3,5},{4,2},{5,3},{6,0},{7,1},{8,14},{9,15},{10,... | collective-permute-start | bytes 786440 | tf_op jit(solution)/shard_map/ppermute | solution.py:343
  3.9 0.5 %collective-permute-start.1 = (bf16[128,1024]{1,0:T(8,128)(2,1)}, bf16[128,1024]{1,0:T(8,128)(2,1)S(1)}, u32[]{:S(2)}, u32[]{:S(2)}) collective-permute-start(bf16[128,1024]{1,0:T(8,128)(2,1)} %o.1), channel_id=1, source_target_pairs={{0,4},{1,3},{2,6},{3,1},{4,0},{5,7},{6,2},{7,5},{8,12},{9,11},{10,... | collective-permute-start | bytes 786440 | tf_op jit(solution)/shard_map/ppermute | solution.py:347
  4.4 0.1 collective-permute-start
  4.5 0.0 collective-permute-done.3.s
  4.5 11.8 %first_kernel.1 = (f32[2,128,1024]{2,1,0:T(8,128)S(1)}, f32[128,1024]{1,0:T(8,128)S(1)}, f32[128,128]{1,0:T(8,128)S(1)}, f32[16,8,128]{2,1,0:T(8,128)S(1)}, f32[...) custom-call(bf16[128,1024]{1,0:T(8,128)(2,1)} %o.1, ...), custom_call_target="tpu_custom_call" | custom-call | flops 1073741824 | tf_op jit(solution)/shard_map/first_kernel/pallas_call | solution.py:350
  16.3 0.0 collective-permute-done.2.d
  16.3 0.4 %collective-permute-done.1.b = bf16[128,1024]{1,0:T(8,128)(2,1)S(1)} collective-permute-done((bf16[128,1024]{1,0:T(8,128)(2,1)}, bf16[128,1024]{1,0:T(8,128)(2,1)S(1)}, u32[]{:S(2)}, u32[]{:S(2)}) %collective-permute-start.1) | collective-permute-done | bytes 262176 | tf_op jit(solution)/shard_map/ppermute | solution.py:347
  16.7 0.3 collective-permute-done.a
  17.0 0.0 collective-permute-start.4
  17.0 0.5 %collective-permute-start.5 = (bf16[128,1024]{1,0:T(8,128)(2,1)S(1)}, bf16[128,1024]{1,0:T(8,128)(2,1)S(1)}, u32[]{:S(2)}, u32[]{:S(2)}) collective-permute-start(bf16[128,1024]{1,0:T(8,128)(2,1)S(1)} %collective-permute-done.1.b), channel_id=1, source_target_pairs={{0,1},{1,0},{2,3},{3,2},{4,5},{5,4},{6,7},{7,6},{8,9},{9,8},{10,11... | collective-permute-start | bytes 786440 | tf_op jit(solution)/shard_map/ppermute | solution.py:343
  17.5 0.0 collective-permute-start.6
  17.5 2.2 %near_kernel.1 = (f32[2,128,1024]{2,1,0:T(8,128)S(1)}, f32[128,128]{1,0:T(8,128)S(1)}, bf16[2,1024,1024]{2,1,0:T(8,128)(2,1)S(1)}) custom-call(bf16[128,1024]{1,0:T(8,128)(2,1)S(1)} %collective-permute-done.a, bf16[128,1024]{1,0:T(8,128)(2,1)S(1)} %collective-permute-done.1.b, bf16[128,1024]{1,0:T(8,128)(2,1)S(1)} %collective-permute-done.2.d, ...), custom_call_target="tpu_custom_call" | custom-call | flops 1610612736 | tf_op jit(solution)/shard_map/near_kernel/pallas_call | solution.py:350
  19.8 0.0 collective-permute-done.4.a.ao
  19.8 0.0 collective-permute-done.5.b.bo
  19.8 0.0 collective-permute-done.6.d.do
  19.8 0.0 copy-start
  19.8 3.2 %far_kernel.1 = (f32[128,128]{1,0:T(8,128)S(1)}, f32[128,8,128]{2,1,0:T(8,128)S(1)}, f32[16,8,128]{2,1,0:T(8,128)S(1)}, bf16[1,3072,1024]{2,1,0:T(8,128)(2,1)S(1)}) custom-call(bf16[128,1024]{1,0:T(8,128)(2,1)S(1)} %collective-permute-done.4.a.ao, bf16[128,1024]{1,0:T(8,128)(2,1)S(1)} %collective-permute-done.5.b.bo, ...), custom_call_target="tpu_custom_call" | custom-call | flops 1610612736 | tf_op jit(solution)/shard_map/far_kernel/pallas_call | solution.py:350
  23.1 1.6 %collective-permute-start.7 = (f32[16,8,128]{2,1,0:T(8,128)S(1)}, f32[16,8,128]{2,1,0:T(8,128)S(1)}, u32[]{:S(2)}, u32[]{:S(2)}) collective-permute-start(f32[16,8,128]{2,1,0:T(8,128)S(1)} %get-tuple-element.43), channel_id=1, source_target_pairs={{0,8},{8,16},{16,24},{24,0},{1,9},{9,17},{17,25},{25,1},{2,10},{10... | collective-permute-start | bytes 196616 | tf_op jit(solution)/shard_map/ppermute | solution.py:411
  24.7 2.6 %collective-permute-start.8 = (bf16[16,8,128]{2,1,0:T(8,128)(2,1)S(1)}, bf16[16,8,128]{2,1,0:T(8,128)(2,1)S(1)}, u32[]{:S(2)}, u32[]{:S(2)}) collective-permute-start(bf16[16,8,128]{2,1,0:T(8,128)(2,1)S(1)} %convert_element_type.3), channel_id=1, source_target_pairs={{0,16},{8,24},{16,0},{24,8},{1,17},{9,25},{17,1},{25,9},{2,18},{10... | collective-permute-start | bytes 98312 | tf_op jit(solution)/shard_map/ppermute | solution.py:411
  27.3 0.0 copy-done
  27.3 3.4 %outer_kernel.1 = (f32[128,1024]{1,0:T(8,128)S(1)}, f32[128,8,128]{2,1,0:T(8,128)S(1)}) custom-call(bf16[128,1024]{1,0:T(8,128)(2,1)S(1)} %collective-permute-done.a, bf16[128,1024]{1,0:T(8,128)(2,1)S(1)} %collective-permute-done.1.b, bf16[128,1024]{1,0:T(8,128)(2,1)S(1)} %collective-permute-done.2.d, bf16[128,1024]{1,0:T(8,128)(2,1)S(1)} %collective-permute-done.4.a.ao, ...), custom_call_target="tpu_custom_call" | custom-call | flops 2147483648 | tf_op jit(solution)/shard_map/outer_kernel/pallas_call | solution.py:350
  30.7 0.2 collective-permute-done.8.refs_1_
  30.9 0.0 collective-permute-done.7.refs_0_
  30.9 1.0 %last.1 = bf16[128,1024]{1,0:T(8,128)(2,1)} custom-call(f32[16,8,128]{2,1,0:T(8,128)S(1)} %collective-permute-done.7.refs_0_, bf16[16,8,128]{2,1,0:T(8,128)(2,1)S(1)} %collective-permute-done.8.refs_1_, f32[128,1024]{1,0:T(8,128)S(1)} %get-tuple-element.49.refs_2_, f32[128,8,128]{2,1,0:T(8,128)S(1)} %get-tuple-element.50.refs_3_, ...), custom_call_target="tpu_custom_call" | custom-call | tf_op jit(solution)/shard_map/last/pallas_call | solution.py:424
  (1 shorter events, 0.0 us)
Async XLA Ops:
  0.0 4.5 %collective-permute-start.3 = (bf16[128,1024]{1,0:T(8,128)(2,1)}, bf16[128,1024]{1,0:T(8,128)(2,1)S(1)}, u32[]{:S(2)}, u32[]{:S(2)}) collective-permute-start(bf16[128,1024]{1,0:T(8,128)(2,1)} %o.1), channel_id=1, source_target_pairs={{0,1},{1,0},{2,3},{3,2},{4,5},{5,4},{6,7},{7,6},{8,9},{9,8},{10,11... | collective-permute-start | bytes 786440 | tf_op jit(solution)/shard_map/ppermute | solution.py:343
  0.5 15.9 %collective-permute-start.2 = (bf16[128,1024]{1,0:T(8,128)(2,1)}, bf16[128,1024]{1,0:T(8,128)(2,1)S(1)}, u32[]{:S(2)}, u32[]{:S(2)}) collective-permute-start(bf16[128,1024]{1,0:T(8,128)(2,1)} %o.1), channel_id=1, source_target_pairs={{0,6},{1,7},{2,4},{3,5},{4,2},{5,3},{6,0},{7,1},{8,14},{9,15},{10,... | collective-permute-start | bytes 786440 | tf_op jit(solution)/shard_map/ppermute | solution.py:343
  3.9 12.8 %collective-permute-start.1 = (bf16[128,1024]{1,0:T(8,128)(2,1)}, bf16[128,1024]{1,0:T(8,128)(2,1)S(1)}, u32[]{:S(2)}, u32[]{:S(2)}) collective-permute-start(bf16[128,1024]{1,0:T(8,128)(2,1)} %o.1), channel_id=1, source_target_pairs={{0,4},{1,3},{2,6},{3,1},{4,0},{5,7},{6,2},{7,5},{8,12},{9,11},{10,... | collective-permute-start | bytes 786440 | tf_op jit(solution)/shard_map/ppermute | solution.py:347
  4.4 12.6 %collective-permute-start = (bf16[128,1024]{1,0:T(8,128)(2,1)}, bf16[128,1024]{1,0:T(8,128)(2,1)S(1)}, u32[]{:S(2)}, u32[]{:S(2)}) collective-permute-start(bf16[128,1024]{1,0:T(8,128)(2,1)} %o.1), channel_id=1, source_target_pairs={{0,2},{1,5},{2,0},{3,7},{4,6},{5,1},{6,4},{7,3},{8,10},{9,13},{10,... | collective-permute-start | bytes 786440 | tf_op jit(solution)/shard_map/ppermute | solution.py:347
  17.0 2.8 %collective-permute-start.4 = (bf16[128,1024]{1,0:T(8,128)(2,1)S(1)}, bf16[128,1024]{1,0:T(8,128)(2,1)S(1)}, u32[]{:S(2)}, u32[]{:S(2)}) collective-permute-start(bf16[128,1024]{1,0:T(8,128)(2,1)S(1)} %collective-permute-done.a), channel_id=1, source_target_pairs={{0,1},{1,0},{2,3},{3,2},{4,5},{5,4},{6,7},{7,6},{8,9},{9,8},{10,11... | collective-permute-start | bytes 786440 | tf_op jit(solution)/shard_map/ppermute | solution.py:343
  17.0 2.8 %collective-permute-start.5 = (bf16[128,1024]{1,0:T(8,128)(2,1)S(1)}, bf16[128,1024]{1,0:T(8,128)(2,1)S(1)}, u32[]{:S(2)}, u32[]{:S(2)}) collective-permute-start(bf16[128,1024]{1,0:T(8,128)(2,1)S(1)} %collective-permute-done.1.b), channel_id=1, source_target_pairs={{0,1},{1,0},{2,3},{3,2},{4,5},{5,4},{6,7},{7,6},{8,9},{9,8},{10,11... | collective-permute-start | bytes 786440 | tf_op jit(solution)/shard_map/ppermute | solution.py:343
  17.5 2.3 %collective-permute-start.6 = (bf16[128,1024]{1,0:T(8,128)(2,1)S(1)}, bf16[128,1024]{1,0:T(8,128)(2,1)S(1)}, u32[]{:S(2)}, u32[]{:S(2)}) collective-permute-start(bf16[128,1024]{1,0:T(8,128)(2,1)S(1)} %collective-permute-done.2.d), channel_id=1, source_target_pairs={{0,1},{1,0},{2,3},{3,2},{4,5},{5,4},{6,7},{7,6},{8,9},{9,8},{10,11... | collective-permute-start | bytes 786440 | tf_op jit(solution)/shard_map/ppermute | solution.py:343
  19.8 7.5 %copy-start = (f32[1024]{0:T(1024)S(1)}, f32[1024]{0:T(1024)}, u32[]{:S(2)}) copy-start(f32[1024]{0:T(1024)} %param.10) | copy-start | bytes 12292
  23.1 7.8 %collective-permute-start.7 = (f32[16,8,128]{2,1,0:T(8,128)S(1)}, f32[16,8,128]{2,1,0:T(8,128)S(1)}, u32[]{:S(2)}, u32[]{:S(2)}) collective-permute-start(f32[16,8,128]{2,1,0:T(8,128)S(1)} %get-tuple-element.43), channel_id=1, source_target_pairs={{0,8},{8,16},{16,24},{24,0},{1,9},{9,17},{17,25},{25,1},{2,10},{10... | collective-permute-start | bytes 196616 | tf_op jit(solution)/shard_map/ppermute | solution.py:411
  24.7 6.2 %collective-permute-start.8 = (bf16[16,8,128]{2,1,0:T(8,128)(2,1)S(1)}, bf16[16,8,128]{2,1,0:T(8,128)(2,1)S(1)}, u32[]{:S(2)}, u32[]{:S(2)}) collective-permute-start(bf16[16,8,128]{2,1,0:T(8,128)(2,1)S(1)} %convert_element_type.3), channel_id=1, source_target_pairs={{0,16},{8,24},{16,0},{24,8},{1,17},{9,25},{17,1},{25,9},{2,18},{10... | collective-permute-start | bytes 98312 | tf_op jit(solution)/shard_map/ppermute | solution.py:411

commit v4 on v3

--- a/solution.py
+++ b/solution.py
@@ -128,18 +128,18 @@
 
 def own_masks():
     core = lax.axis_index("ch") & 1
-    one, two = 2 + 2 * core, 4 - 2 * core
+    one, two = 4 - 2 * core, 2 + 2 * core
     return (one, two, 6)
 
 
 def other_masks():
     core = lax.axis_index("ch") & 1
-    one, two = 2 + 2 * core, 4 - 2 * core
+    one, two = 4 - 2 * core, 2 + 2 * core
     return (two ^ 1, one ^ 1, 7)
 
 
 def first_kernel(
-    o, s, wt, rate, res, lengths, acc, outer, sq, lam3, mix3, near, far, gate, rowmask, valid, held, wbuf, gbuf, rates, ress, docs, sem, small
+    o, s, wt, rate, res, lengths, acc, outer, sq, lam3, mix3, near, far, rowmask, valid, held, wbuf, gbuf, rates, ress, docs, sem, small
 ):
     rows, depth = s.shape
     own = [
@@ -152,7 +152,6 @@
     copies += weight_copies(wt, GATE, (0, 1), depth, gbuf, sem, 4)
     copies += weight_copies(wt, DRIVEN, own_masks(), depth, near, sem, 6)
     copies += weight_copies(wt, DRIVEN, other_masks()[:2], depth, far, sem, 12)
-    copies += weight_copies(wt, GATE, own_masks()[:1], depth, gate, sem, 16)
     run_copies(own, len(own))
     wait = run_copies(copies, 8)
     for c in own:
@@ -198,7 +197,7 @@
 
 
 def far_kernel(
-    a, b, d, weights, last_weights, wt, acc_in, sq_in, lam3, rowmask, scale, d3, e3, gate, both, sem
+    weights, a, b, d, last_weights, wt, acc_in, sq_in, lam3, rowmask, scale, d3, e3, gate, both, sem
 ):
     rows, depth = a.shape
     wait = run_copies(weight_copies(wt, GATE, own_masks()[1:] + other_masks()[:1], depth, gate, sem), 8)
@@ -260,11 +259,11 @@
 
 
 def outer_kernel(
-    a, b, d, ao, bo, do, wt, sum_in, gate_a, gate_far, d3, lam3, mix3, skip, rowmask, outer, f3, wbuf, sem
+    a, b, d, ao, bo, do, wt, sum_in, gate_far, d3, lam3, mix3, skip, rowmask, outer, f3, wbuf, sem
 ):
     rows, depth = a.shape
     modes = lam3.shape[0]
-    wait = run_copies(weight_copies(wt, GATE, other_masks()[1:], depth, wbuf, sem), 8)
+    wait = run_copies(weight_copies(wt, GATE, own_masks()[:1] + other_masks()[1:], depth, wbuf, sem), 8)
 
     def body(step, state):
         first = pl.multiple_of(step * SUB, SUB)
@@ -280,10 +279,11 @@
 
     zeros = [jnp.zeros((SUB, LANE), jnp.float32) for _ in range(modes)]
     lax.fori_loop(0, rows // SUB, body, zeros)
-    total = sum_in[...] + project((a,), gate_a, 0) + project((b, d, ao), gate_far, 0)
-    wait(0)
-    wait(1)
-    outer[...] = total + project((bo, do), wbuf, 0)
+    total = sum_in[...] + project((b, d, ao), gate_far, 0)
+    for i, block in enumerate((a, bo, do)):
+        wait(i)
+        total = total + dot(block[...], wbuf[0, i * depth : (i + 1) * depth])
+    outer[...] = total
 
 
 def last_kernel(*refs, count):
@@ -343,7 +343,7 @@
         return lax.ppermute(block, "ch", [(i, i ^ mask) for i in range(size)])
 
     def split(block, first):
-        masks = (2, 4) if first else (4, 2)
+        masks = (4, 2) if first else (2, 4)
         return lax.ppermute(block, "ch", [(i, i ^ masks[i & 1]) for i in range(size)])
 
     def call(kernel, ins, outs, scratch, flops, mib):
@@ -379,12 +379,12 @@
 
     s = swap(stream, 1)
     a, b, d = split(stream, True), split(stream, False), swap(stream, 6)
-    acc, outer, sq, lam3, mix3, near, far, gate_a, rowmask, valid = call(
+    acc, outer, sq, lam3, mix3, near, far, rowmask, valid = call(
         first_kernel,
         there(stream) + here(s) + there(wt, rate, res, doc_lengths),
-        [planes, product, squares, poles, poles, weights(2, 3), weights(2, 2), weights(1, 1)]
+        [planes, product, squares, poles, poles, weights(2, 3), weights(2, 2)]
         + [pltpu.VMEM((3, rows, LANE), f32), pltpu.VMEM((reach, SUB, LANE), f32)],
-        [chunk, weights(2, 2), weights(1, 2), vector, vector, pltpu.SMEM(doc_lengths.shape, jnp.int32), dma((17,)), dma((4,))],
+        [chunk, weights(2, 2), weights(1, 2), vector, vector, pltpu.SMEM(doc_lengths.shape, jnp.int32), dma((16,)), dma((4,))],
         4,
         16,
     )
@@ -400,7 +400,7 @@
     )
     scale, d3, e3, gate_far = call(
         far_kernel,
-        here(ao, bo, do, far, far_d) + there(wt) + here(acc, sq, lam3, rowmask),
+        here(far, ao, bo, do, far_d) + there(wt) + here(acc, sq, lam3, rowmask),
         [squares, tokens, poles, weights(1, 3)],
         [planes, dma((3,))],
         6,
@@ -415,10 +415,10 @@
         outer_kernel,
         here(a, b, d, ao, bo, do)
         + there(wt)
-        + here(outer, gate_a, gate_far, d3, lam3, mix3, skip_gain.reshape(SUB, LANE), rowmask),
+        + here(outer, gate_far, d3, lam3, mix3, skip_gain.reshape(SUB, LANE), rowmask),
         [product, tokens],
-        [weights(1, 2), dma((2,))],
-        8,
+        [weights(1, 3), dma((3,))],
+        6,
         16,
     )
     return pl.pallas_call(

time: 32.1 us -> 31.4 us (0.978)
  waiting for transfers between devices: 0.86 us -> 0.1 us
  starting transfers between devices: 9.27 us -> 9.73 us
  Pallas kernels: 21.7 us -> 21.3 us
    ppermute x2, starting transfers between devices: 0.63 us -> 2.62 us  [split(): lax.ppermute(block, 'ch', [(i, i ^ masks[i & 1]) for i in range(size)])]
    ppermute x5, starting transfers between devices: 4.41 us -> 2.51 us  [swap(): return lax.ppermute(block, 'ch', [(i, i ^ mask) for i in range(size)])]
    ppermute x2, waiting for transfers between devices: 0.66 us -> 0.09 us  [split(): lax.ppermute(block, 'ch', [(i, i ^ masks[i & 1]) for i in range(size)])]
    pallas_call x4, Pallas kernels: 20.7 us -> 20.2 us  [call(): pl.pallas_call(kernel, in_specs=[spec for spec, _ in ins], out_specs=[IN_...]
    ppermute x2, starting transfers between devices: 4.23 us -> 4.61 us  [fitted(): lax.ppermute(e3 if k == 1 else e3.astype(b16), 'ctx', [(i, (i + k) % ring...]
  transfers between devices with their start and end apart: 9 -> 9, of which waited for: 3 -> 1; matrix products, arithmetic and copies ran while one was open for 0% -> 0% of each run, Pallas kernels for 54% -> 54%
where the time goes in v4:
time: 31.4 us; the launch traced here: 31.2 us
  Pallas kernels  21.3 us (68%)
  starting transfers between devices  9.73 us (31%)
    pallas_call x4, Pallas kernels, call(): pl.pallas_call(kernel, in_specs=[spec for spec, _ in ins], out_specs=[IN_...  20.2 us
    ppermute x2, starting transfers between devices, fitted(): lax.ppermute(e3 if k == 1 else e3.astype(b16), 'ctx', [(i, (i + k) % ring...  4.61 us
    ppermute x2, starting transfers between devices, split(): lax.ppermute(block, 'ch', [(i, i ^ masks[i & 1]) for i in range(size)])  2.62 us
    ppermute x5, starting transfers between devices, swap(): return lax.ppermute(block, 'ch', [(i, i ^ mask) for i in range(size)])  2.51 us
    pallas_call x1, Pallas kernels, fitted(): pl.pallas_call(functools.partial(last_kernel, count=reach), in_specs=[IN_...  1.06 us
  transfers between devices with their start and end apart: 9, of which 1 were waited for; matrix products, arithmetic and copies ran while one was open for 0% of the time, Pallas kernels for 54%

profile of v4, /device:TPU:0, one launch (start us, length us, event | category | flops | bytes accessed | tf_op | source)
XLA Modules:
  0.0 31.2 jit_solution(3209719190391703931)
XLA Ops:
  0.0 0.5 %collective-permute-start = (bf16[128,1024]{1,0:T(8,128)(2,1)}, bf16[128,1024]{1,0:T(8,128)(2,1)S(1)}, u32[]{:S(2)}, u32[]{:S(2)}) collective-permute-start(bf16[128,1024]{1,0:T(8,128)(2,1)} %o.1), channel_id=1, source_target_pairs={{0,1},{1,0},{2,3},{3,2},{4,5},{5,4},{6,7},{7,6},{8,9},{9,8},{10,11... | collective-permute-start | bytes 786440 | tf_op jit(solution)/shard_map/ppermute | solution.py:343
  0.5 2.5 %collective-permute-start.1 = (bf16[128,1024]{1,0:T(8,128)(2,1)}, bf16[128,1024]{1,0:T(8,128)(2,1)S(1)}, u32[]{:S(2)}, u32[]{:S(2)}) collective-permute-start(bf16[128,1024]{1,0:T(8,128)(2,1)} %o.1), channel_id=1, source_target_pairs={{0,4},{1,3},{2,6},{3,1},{4,0},{5,7},{6,2},{7,5},{8,12},{9,11},{10,... | collective-permute-start | bytes 786440 | tf_op jit(solution)/shard_map/ppermute | solution.py:347
  3.0 1.4 %collective-permute-start.3 = (bf16[128,1024]{1,0:T(8,128)(2,1)}, bf16[128,1024]{1,0:T(8,128)(2,1)S(1)}, u32[]{:S(2)}, u32[]{:S(2)}) collective-permute-start(bf16[128,1024]{1,0:T(8,128)(2,1)} %o.1), channel_id=1, source_target_pairs={{0,6},{1,7},{2,4},{3,5},{4,2},{5,3},{6,0},{7,1},{8,14},{9,15},{10,... | collective-permute-start | bytes 786440 | tf_op jit(solution)/shard_map/ppermute | solution.py:343
  4.4 0.1 collective-permute-start.2
  4.5 0.0 collective-permute-done.s
  4.5 11.2 %first_kernel.1 = (f32[2,128,1024]{2,1,0:T(8,128)S(1)}, f32[128,1024]{1,0:T(8,128)S(1)}, f32[128,128]{1,0:T(8,128)S(1)}, f32[16,8,128]{2,1,0:T(8,128)S(1)}, f32[...) custom-call(bf16[128,1024]{1,0:T(8,128)(2,1)} %o.1, ...), custom_call_target="tpu_custom_call" | custom-call | flops 1073741824 | tf_op jit(solution)/shard_map/first_kernel/pallas_call | solution.py:350
  15.7 0.0 collective-permute-done.1.a
  15.7 0.0 collective-permute-done.3.d
  15.7 0.1 collective-permute-done.2.b
  15.8 0.1 collective-permute-start.4
  15.9 0.4 %collective-permute-start.5 = (bf16[128,1024]{1,0:T(8,128)(2,1)S(1)}, bf16[128,1024]{1,0:T(8,128)(2,1)S(1)}, u32[]{:S(2)}, u32[]{:S(2)}) collective-permute-start(bf16[128,1024]{1,0:T(8,128)(2,1)S(1)} %collective-permute-done.2.b), channel_id=1, source_target_pairs={{0,1},{1,0},{2,3},{3,2},{4,5},{5,4},{6,7},{7,6},{8,9},{9,8},{10,11... | collective-permute-start | bytes 786440 | tf_op jit(solution)/shard_map/ppermute | solution.py:343
  16.3 0.1 collective-permute-start.6
  16.4 2.2 %near_kernel.1 = (f32[2,128,1024]{2,1,0:T(8,128)S(1)}, f32[128,128]{1,0:T(8,128)S(1)}, bf16[2,1024,1024]{2,1,0:T(8,128)(2,1)S(1)}) custom-call(bf16[128,1024]{1,0:T(8,128)(2,1)S(1)} %collective-permute-done.1.a, bf16[128,1024]{1,0:T(8,128)(2,1)S(1)} %collective-permute-done.2.b, bf16[128,1024]{1,0:T(8,128)(2,1)S(1)} %collective-permute-done.3.d, ...), custom_call_target="tpu_custom_call" | custom-call | flops 1610612736 | tf_op jit(solution)/shard_map/near_kernel/pallas_call | solution.py:350
  18.7 0.0 collective-permute-done.4.a.ao
  18.7 0.0 collective-permute-done.5.b.bo
  18.7 0.0 collective-permute-done.6.d.do
  18.7 0.0 copy-start
  18.7 3.2 %far_kernel.1 = (f32[128,128]{1,0:T(8,128)S(1)}, f32[128,8,128]{2,1,0:T(8,128)S(1)}, f32[16,8,128]{2,1,0:T(8,128)S(1)}, bf16[1,3072,1024]{2,1,0:T(8,128)(2,1)S(1)}) custom-call(bf16[2,2048,1024]{2,1,0:T(8,128)(2,1)S(1)} %get-tuple-element.28.weights, bf16[128,1024]{1,0:T(8,128)(2,1)S(1)} %collective-permute-done.4.a.ao, ...), custom_call_target="tpu_custom_call" | custom-call | flops 1610612736 | tf_op jit(solution)/shard_map/far_kernel/pallas_call | solution.py:350
  22.0 2.0 %collective-permute-start.7 = (f32[16,8,128]{2,1,0:T(8,128)S(1)}, f32[16,8,128]{2,1,0:T(8,128)S(1)}, u32[]{:S(2)}, u32[]{:S(2)}) collective-permute-start(f32[16,8,128]{2,1,0:T(8,128)S(1)} %get-tuple-element.42), channel_id=1, source_target_pairs={{0,8},{8,16},{16,24},{24,0},{1,9},{9,17},{17,25},{25,1},{2,10},{10... | collective-permute-start | bytes 196616 | tf_op jit(solution)/shard_map/ppermute | solution.py:411
  24.0 2.6 %collective-permute-start.8 = (bf16[16,8,128]{2,1,0:T(8,128)(2,1)S(1)}, bf16[16,8,128]{2,1,0:T(8,128)(2,1)S(1)}, u32[]{:S(2)}, u32[]{:S(2)}) collective-permute-start(bf16[16,8,128]{2,1,0:T(8,128)(2,1)S(1)} %convert_element_type.3), channel_id=1, source_target_pairs={{0,16},{8,24},{16,0},{24,8},{1,17},{9,25},{17,1},{25,9},{2,18},{10... | collective-permute-start | bytes 98312 | tf_op jit(solution)/shard_map/ppermute | solution.py:411
  26.6 0.0 copy-done
  26.6 3.5 %outer_kernel.1 = (f32[128,1024]{1,0:T(8,128)S(1)}, f32[128,8,128]{2,1,0:T(8,128)S(1)}) custom-call(bf16[128,1024]{1,0:T(8,128)(2,1)S(1)} %collective-permute-done.1.a, bf16[128,1024]{1,0:T(8,128)(2,1)S(1)} %collective-permute-done.2.b, bf16[128,1024]{1,0:T(8,128)(2,1)S(1)} %collective-permute-done.3.d, bf16[128,1024]{1,0:T(8,128)(2,1)S(1)} %collective-permute-done.4.a.ao, ...), custom_call_target="tpu_custom_call" | custom-call | flops 1610612736 | tf_op jit(solution)/shard_map/outer_kernel/pallas_call | solution.py:350
  30.1 0.0 collective-permute-done.8.refs_1_
  30.2 0.0 collective-permute-done.7.refs_0_
  30.2 1.1 %last.1 = bf16[128,1024]{1,0:T(8,128)(2,1)} custom-call(f32[16,8,128]{2,1,0:T(8,128)S(1)} %collective-permute-done.7.refs_0_, bf16[16,8,128]{2,1,0:T(8,128)(2,1)S(1)} %collective-permute-done.8.refs_1_, f32[128,1024]{1,0:T(8,128)S(1)} %get-tuple-element.47.refs_2_, f32[128,8,128]{2,1,0:T(8,128)S(1)} %get-tuple-element.48.refs_3_, ...), custom_call_target="tpu_custom_call" | custom-call | tf_op jit(solution)/shard_map/last/pallas_call | solution.py:424
  (1 shorter events, 0.0 us)
Async XLA Ops:
  0.0 4.5 %collective-permute-start = (bf16[128,1024]{1,0:T(8,128)(2,1)}, bf16[128,1024]{1,0:T(8,128)(2,1)S(1)}, u32[]{:S(2)}, u32[]{:S(2)}) collective-permute-start(bf16[128,1024]{1,0:T(8,128)(2,1)} %o.1), channel_id=1, source_target_pairs={{0,1},{1,0},{2,3},{3,2},{4,5},{5,4},{6,7},{7,6},{8,9},{9,8},{10,11... | collective-permute-start | bytes 786440 | tf_op jit(solution)/shard_map/ppermute | solution.py:343
  0.5 15.2 %collective-permute-start.1 = (bf16[128,1024]{1,0:T(8,128)(2,1)}, bf16[128,1024]{1,0:T(8,128)(2,1)S(1)}, u32[]{:S(2)}, u32[]{:S(2)}) collective-permute-start(bf16[128,1024]{1,0:T(8,128)(2,1)} %o.1), channel_id=1, source_target_pairs={{0,4},{1,3},{2,6},{3,1},{4,0},{5,7},{6,2},{7,5},{8,12},{9,11},{10,... | collective-permute-start | bytes 786440 | tf_op jit(solution)/shard_map/ppermute | solution.py:347
  3.0 12.7 %collective-permute-start.3 = (bf16[128,1024]{1,0:T(8,128)(2,1)}, bf16[128,1024]{1,0:T(8,128)(2,1)S(1)}, u32[]{:S(2)}, u32[]{:S(2)}) collective-permute-start(bf16[128,1024]{1,0:T(8,128)(2,1)} %o.1), channel_id=1, source_target_pairs={{0,6},{1,7},{2,4},{3,5},{4,2},{5,3},{6,0},{7,1},{8,14},{9,15},{10,... | collective-permute-start | bytes 786440 | tf_op jit(solution)/shard_map/ppermute | solution.py:343
  4.4 11.4 %collective-permute-start.2 = (bf16[128,1024]{1,0:T(8,128)(2,1)}, bf16[128,1024]{1,0:T(8,128)(2,1)S(1)}, u32[]{:S(2)}, u32[]{:S(2)}) collective-permute-start(bf16[128,1024]{1,0:T(8,128)(2,1)} %o.1), channel_id=1, source_target_pairs={{0,2},{1,5},{2,0},{3,7},{4,6},{5,1},{6,4},{7,3},{8,10},{9,13},{10,... | collective-permute-start | bytes 786440 | tf_op jit(solution)/shard_map/ppermute | solution.py:347
  15.8 2.9 %collective-permute-start.4 = (bf16[128,1024]{1,0:T(8,128)(2,1)S(1)}, bf16[128,1024]{1,0:T(8,128)(2,1)S(1)}, u32[]{:S(2)}, u32[]{:S(2)}) collective-permute-start(bf16[128,1024]{1,0:T(8,128)(2,1)S(1)} %collective-permute-done.1.a), channel_id=1, source_target_pairs={{0,1},{1,0},{2,3},{3,2},{4,5},{5,4},{6,7},{7,6},{8,9},{9,8},{10,11... | collective-permute-start | bytes 786440 | tf_op jit(solution)/shard_map/ppermute | solution.py:343
  15.9 2.8 %collective-permute-start.5 = (bf16[128,1024]{1,0:T(8,128)(2,1)S(1)}, bf16[128,1024]{1,0:T(8,128)(2,1)S(1)}, u32[]{:S(2)}, u32[]{:S(2)}) collective-permute-start(bf16[128,1024]{1,0:T(8,128)(2,1)S(1)} %collective-permute-done.2.b), channel_id=1, source_target_pairs={{0,1},{1,0},{2,3},{3,2},{4,5},{5,4},{6,7},{7,6},{8,9},{9,8},{10,11... | collective-permute-start | bytes 786440 | tf_op jit(solution)/shard_map/ppermute | solution.py:343
  16.3 2.4 %collective-permute-start.6 = (bf16[128,1024]{1,0:T(8,128)(2,1)S(1)}, bf16[128,1024]{1,0:T(8,128)(2,1)S(1)}, u32[]{:S(2)}, u32[]{:S(2)}) collective-permute-start(bf16[128,1024]{1,0:T(8,128)(2,1)S(1)} %collective-permute-done.3.d), channel_id=1, source_target_pairs={{0,1},{1,0},{2,3},{3,2},{4,5},{5,4},{6,7},{7,6},{8,9},{9,8},{10,11... | collective-permute-start | bytes 786440 | tf_op jit(solution)/shard_map/ppermute | solution.py:343
  18.7 7.9 %copy-start = (f32[1024]{0:T(1024)S(1)}, f32[1024]{0:T(1024)}, u32[]{:S(2)}) copy-start(f32[1024]{0:T(1024)} %param.10) | copy-start | bytes 12292
  22.0 8.2 %collective-permute-start.7 = (f32[16,8,128]{2,1,0:T(8,128)S(1)}, f32[16,8,128]{2,1,0:T(8,128)S(1)}, u32[]{:S(2)}, u32[]{:S(2)}) collective-permute-start(f32[16,8,128]{2,1,0:T(8,128)S(1)} %get-tuple-element.42), channel_id=1, source_target_pairs={{0,8},{8,16},{16,24},{24,0},{1,9},{9,17},{17,25},{25,1},{2,10},{10... | collective-permute-start | bytes 196616 | tf_op jit(solution)/shard_map/ppermute | solution.py:411
  24.0 6.1 %collective-permute-start.8 = (bf16[16,8,128]{2,1,0:T(8,128)(2,1)S(1)}, bf16[16,8,128]{2,1,0:T(8,128)(2,1)S(1)}, u32[]{:S(2)}, u32[]{:S(2)}) collective-permute-start(bf16[16,8,128]{2,1,0:T(8,128)(2,1)S(1)} %convert_element_type.3), channel_id=1, source_target_pairs={{0,16},{8,24},{16,0},{24,8},{1,17},{9,25},{17,1},{25,9},{2,18},{10... | collective-permute-start | bytes 98312 | tf_op jit(solution)/shard_map/ppermute | solution.py:411

commit v5 on v4

--- a/solution.py
+++ b/solution.py
@@ -153,7 +153,7 @@
     copies += weight_copies(wt, DRIVEN, own_masks(), depth, near, sem, 6)
     copies += weight_copies(wt, DRIVEN, other_masks()[:2], depth, far, sem, 12)
     run_copies(own, len(own))
-    wait = run_copies(copies, 8)
+    wait = run_copies(copies, 6)
     for c in own:
         c.wait()
     blocks = (held, s)
@@ -183,9 +183,14 @@
         wait(i)
 
 
-def near_kernel(a, b, d, weights, wt, acc_in, sq_in, acc, sq, far, sem):
-    blocks = (a, b, d)
-    wait = run_copies(weight_copies(wt, DRIVEN, other_masks()[2:], a.shape[1], far, sem), 8)
+def pack_kernel(a, b, d, packed):
+    for i, ref in enumerate((a, b, d)):
+        packed[i] = ref[...]
+
+
+def near_kernel(packed, weights, wt, acc_in, sq_in, acc, sq, far, sem):
+    blocks = [packed.at[i] for i in range(3)]
+    wait = run_copies(weight_copies(wt, DRIVEN, other_masks()[2:], packed.shape[2], far, sem), 8)
     sq[...] = add_squares(sq_in[...], blocks)
 
     @pl.loop(0, 2)
@@ -197,18 +202,18 @@
 
 
 def far_kernel(
-    weights, a, b, d, last_weights, wt, acc_in, sq_in, lam3, rowmask, scale, d3, e3, gate, both, sem
+    weights, packed, last_weights, wt, acc_in, sq_in, lam3, rowmask, scale, d3, e3, gate, both, sem
 ):
-    rows, depth = a.shape
+    _, rows, depth = packed.shape
     wait = run_copies(weight_copies(wt, GATE, own_masks()[1:] + other_masks()[:1], depth, gate, sem), 8)
-    blocks = (a, b, d)
+    blocks = [packed.at[i] for i in range(3)]
     total = jnp.sum(add_squares(sq_in[...], blocks), axis=1, keepdims=True)
     row = lax.rsqrt(total / (8 * depth) + 1e-06)
     scale[...] = jnp.broadcast_to(row, scale.shape)
 
     @pl.loop(0, 2)
     def _(k):
-        both[k] = acc_in[k] + project((a, b), weights, k) + project((d,), last_weights, k)
+        both[k] = acc_in[k] + project(blocks[:2], weights, k) + project(blocks[2:], last_weights, k)
 
     for g in range(SUB):
         cols = slice(g * LANE, (g + 1) * LANE)
@@ -259,9 +264,11 @@
 
 
 def outer_kernel(
-    a, b, d, ao, bo, do, wt, sum_in, gate_far, d3, lam3, mix3, skip, rowmask, outer, f3, wbuf, sem
+    own, others, wt, sum_in, gate_far, d3, lam3, mix3, skip, rowmask, outer, f3, wbuf, sem
 ):
-    rows, depth = a.shape
+    _, rows, depth = own.shape
+    a, b, d = [own.at[i] for i in range(3)]
+    ao, bo, do = [others.at[i] for i in range(3)]
     modes = lam3.shape[0]
     wait = run_copies(weight_copies(wt, GATE, own_masks()[:1] + other_masks()[1:], depth, wbuf, sem), 8)
 
@@ -389,10 +396,11 @@
         16,
     )
     a, b, d, acc, sq = lax.optimization_barrier((a, b, d, acc, sq))
-    ao, bo, do = swap(a, 1), swap(b, 1), swap(d, 1)
+    (own,) = call(pack_kernel, here(a, b, d), [pltpu.VMEM((3, rows, depth), b16)], [], 1, 1)
+    others = swap(own, 1)
     acc, sq, far_d = call(
         near_kernel,
-        here(a, b, d, near) + there(wt) + here(acc, sq),
+        here(own, near) + there(wt) + here(acc, sq),
         [planes, squares, weights(2, 1)],
         [dma((2,))],
         6,
@@ -400,7 +408,7 @@
     )
     scale, d3, e3, gate_far = call(
         far_kernel,
-        here(far, ao, bo, do, far_d) + there(wt) + here(acc, sq, lam3, rowmask),
+        here(far, others, far_d) + there(wt) + here(acc, sq, lam3, rowmask),
         [squares, tokens, poles, weights(1, 3)],
         [planes, dma((3,))],
         6,
@@ -413,7 +421,7 @@
     ]
     outer, f3 = call(
         outer_kernel,
-        here(a, b, d, ao, bo, do)
+        here(own, others)
         + there(wt)
         + here(outer, gate_far, d3, lam3, mix3, skip_gain.reshape(SUB, LANE), rowmask),
         [product, tokens],

time: 31.4 us -> 31 us (0.987)
  starting transfers between devices: 9.73 us -> 9.29 us
    ppermute x5 -> x3, starting transfers between devices: 2.51 us -> 2.07 us  [swap(): return lax.ppermute(block, 'ch', [(i, i ^ mask) for i in range(size)])]
    pallas_call x4 -> x5, Pallas kernels: 20.2 us -> 20.2 us  [call(): pl.pallas_call(kernel, in_specs=[spec for spec, _ in ins], out_specs=[IN_...]
  transfers between devices with their start and end apart: 9 -> 7, of which waited for: 1 -> 1; matrix products, arithmetic and copies ran while one was open for 0% -> 0% of each run, Pallas kernels for 54% -> 55%
where the time goes in v5:
time: 31 us; the launch traced here: 30.8 us
  Pallas kernels  21.3 us (69%)
  starting transfers between devices  9.29 us (30%)
    pallas_call x5, Pallas kernels, call(): pl.pallas_call(kernel, in_specs=[spec for spec, _ in ins], out_specs=[IN_...  20.2 us
    ppermute x2, starting transfers between devices, fitted(): lax.ppermute(e3 if k == 1 else e3.astype(b16), 'ctx', [(i, (i + k) % ring...  4.61 us
    ppermute x2, starting transfers between devices, split(): lax.ppermute(block, 'ch', [(i, i ^ masks[i & 1]) for i in range(size)])  2.62 us
    ppermute x3, starting transfers between devices, swap(): return lax.ppermute(block, 'ch', [(i, i ^ mask) for i in range(size)])  2.07 us
    pallas_call x1, Pallas kernels, fitted(): pl.pallas_call(functools.partial(last_kernel, count=reach), in_specs=[IN_...  1.06 us
  transfers between devices with their start and end apart: 7, of which 1 were waited for; matrix products, arithmetic and copies ran while one was open for 0% of the time, Pallas kernels for 55%

profile of v5, /device:TPU:0, one launch (start us, length us, event | category | flops | bytes accessed | tf_op | source)
XLA Modules:
  0.0 30.8 jit_solution(3314543788015161347)
XLA Ops:
  0.0 0.5 %collective-permute-start = (bf16[128,1024]{1,0:T(8,128)(2,1)}, bf16[128,1024]{1,0:T(8,128)(2,1)S(1)}, u32[]{:S(2)}, u32[]{:S(2)}) collective-permute-start(bf16[128,1024]{1,0:T(8,128)(2,1)} %o.1), channel_id=1, source_target_pairs={{0,1},{1,0},{2,3},{3,2},{4,5},{5,4},{6,7},{7,6},{8,9},{9,8},{10,11... | collective-permute-start | bytes 786440 | tf_op jit(solution)/shard_map/ppermute | solution.py:350
  0.5 2.5 %collective-permute-start.1 = (bf16[128,1024]{1,0:T(8,128)(2,1)}, bf16[128,1024]{1,0:T(8,128)(2,1)S(1)}, u32[]{:S(2)}, u32[]{:S(2)}) collective-permute-start(bf16[128,1024]{1,0:T(8,128)(2,1)} %o.1), channel_id=1, source_target_pairs={{0,4},{1,3},{2,6},{3,1},{4,0},{5,7},{6,2},{7,5},{8,12},{9,11},{10,... | collective-permute-start | bytes 786440 | tf_op jit(solution)/shard_map/ppermute | solution.py:354
  3.0 1.4 %collective-permute-start.3 = (bf16[128,1024]{1,0:T(8,128)(2,1)}, bf16[128,1024]{1,0:T(8,128)(2,1)S(1)}, u32[]{:S(2)}, u32[]{:S(2)}) collective-permute-start(bf16[128,1024]{1,0:T(8,128)(2,1)} %o.1), channel_id=1, source_target_pairs={{0,6},{1,7},{2,4},{3,5},{4,2},{5,3},{6,0},{7,1},{8,14},{9,15},{10,... | collective-permute-start | bytes 786440 | tf_op jit(solution)/shard_map/ppermute | solution.py:350
  4.4 0.1 collective-permute-start.2
  4.5 0.0 collective-permute-done.s
  4.5 11.1 %first_kernel.1 = (f32[2,128,1024]{2,1,0:T(8,128)S(1)}, f32[128,1024]{1,0:T(8,128)S(1)}, f32[128,128]{1,0:T(8,128)S(1)}, f32[16,8,128]{2,1,0:T(8,128)S(1)}, f32[...) custom-call(bf16[128,1024]{1,0:T(8,128)(2,1)} %o.1, ...), custom_call_target="tpu_custom_call" | custom-call | flops 1073741824 | tf_op jit(solution)/shard_map/first_kernel/pallas_call | solution.py:357
  15.7 0.0 collective-permute-done.1.a
  15.7 0.0 collective-permute-done.3.d
  15.7 0.1 collective-permute-done.2.b
  15.8 0.1 pack_kernel.1.packed.own
  15.8 0.2 collective-permute-start.4
  16.0 2.2 %near_kernel.1 = (f32[2,128,1024]{2,1,0:T(8,128)S(1)}, f32[128,128]{1,0:T(8,128)S(1)}, bf16[2,1024,1024]{2,1,0:T(8,128)(2,1)S(1)}) custom-call(bf16[3,128,1024]{2,1,0:T(8,128)(2,1)S(1)} %pack_kernel.1.packed.own, bf16[2,3072,1024]{2,1,0:T(8,128)(2,1)S(1)} %get-tuple-element.34.weights, bf16[3,8192,1024]{2,1,0:T(8,128)(2,1)} %bitcast.6, ...), custom_call_target="tpu_custom_call" | custom-call | flops 1610612736 | tf_op jit(solution)/shard_map/near_kernel/pallas_call | solution.py:357
  18.3 0.0 collective-permute-done.4.packed.others
  18.3 0.0 copy-start
  18.3 3.2 %far_kernel.1 = (f32[128,128]{1,0:T(8,128)S(1)}, f32[128,8,128]{2,1,0:T(8,128)S(1)}, f32[16,8,128]{2,1,0:T(8,128)S(1)}, bf16[1,3072,1024]{2,1,0:T(8,128)(2,1)S(1)}) custom-call(bf16[2,2048,1024]{2,1,0:T(8,128)(2,1)S(1)} %get-tuple-element.28.weights, bf16[3,128,1024]{2,1,0:T(8,128)(2,1)S(1)} %collective-permute-done.4.packed.others, ...), custom_call_target="tpu_custom_call" | custom-call | flops 1610612736 | tf_op jit(solution)/shard_map/far_kernel/pallas_call | solution.py:357
  21.6 2.0 %collective-permute-start.5 = (f32[16,8,128]{2,1,0:T(8,128)S(1)}, f32[16,8,128]{2,1,0:T(8,128)S(1)}, u32[]{:S(2)}, u32[]{:S(2)}) collective-permute-start(f32[16,8,128]{2,1,0:T(8,128)S(1)} %get-tuple-element.42), channel_id=1, source_target_pairs={{0,8},{8,16},{16,24},{24,0},{1,9},{9,17},{17,25},{25,1},{2,10},{10... | collective-permute-start | bytes 196616 | tf_op jit(solution)/shard_map/ppermute | solution.py:419
  23.6 2.6 %collective-permute-start.6 = (bf16[16,8,128]{2,1,0:T(8,128)(2,1)S(1)}, bf16[16,8,128]{2,1,0:T(8,128)(2,1)S(1)}, u32[]{:S(2)}, u32[]{:S(2)}) collective-permute-start(bf16[16,8,128]{2,1,0:T(8,128)(2,1)S(1)} %convert_element_type.3), channel_id=1, source_target_pairs={{0,16},{8,24},{16,0},{24,8},{1,17},{9,25},{17,1},{25,9},{2,18},{10... | collective-permute-start | bytes 98312 | tf_op jit(solution)/shard_map/ppermute | solution.py:419
  26.2 0.0 copy-done
  26.2 3.6 %outer_kernel.1 = (f32[128,1024]{1,0:T(8,128)S(1)}, f32[128,8,128]{2,1,0:T(8,128)S(1)}) custom-call(bf16[3,128,1024]{2,1,0:T(8,128)(2,1)S(1)} %pack_kernel.1.packed.own, bf16[3,128,1024]{2,1,0:T(8,128)(2,1)S(1)} %collective-permute-done.4.packed.others, bf16[3,8192,1024]{2,1,0:T(8,128)(2,1)} %bitcast.8, f32[128,1024]{1,0:T(8,128)S(1)} %get-tuple-element.43.sum_in, ...), custom_call_target="tpu_custom_call" | custom-call | flops 1610612736 | tf_op jit(solution)/shard_map/outer_kernel/pallas_call | solution.py:357
  29.8 0.0 collective-permute-done.6.refs_1_
  29.8 0.0 collective-permute-done.5.refs_0_
  29.8 1.1 %last.1 = bf16[128,1024]{1,0:T(8,128)(2,1)} custom-call(f32[16,8,128]{2,1,0:T(8,128)S(1)} %collective-permute-done.5.refs_0_, bf16[16,8,128]{2,1,0:T(8,128)(2,1)S(1)} %collective-permute-done.6.refs_1_, f32[128,1024]{1,0:T(8,128)S(1)} %get-tuple-element.47.refs_2_, f32[128,8,128]{2,1,0:T(8,128)S(1)} %get-tuple-element.48.refs_3_, ...), custom_call_target="tpu_custom_call" | custom-call | tf_op jit(solution)/shard_map/last/pallas_call | solution.py:432
  (1 shorter events, 0.0 us)
Async XLA Ops:
  0.0 4.5 %collective-permute-start = (bf16[128,1024]{1,0:T(8,128)(2,1)}, bf16[128,1024]{1,0:T(8,128)(2,1)S(1)}, u32[]{:S(2)}, u32[]{:S(2)}) collective-permute-start(bf16[128,1024]{1,0:T(8,128)(2,1)} %o.1), channel_id=1, source_target_pairs={{0,1},{1,0},{2,3},{3,2},{4,5},{5,4},{6,7},{7,6},{8,9},{9,8},{10,11... | collective-permute-start | bytes 786440 | tf_op jit(solution)/shard_map/ppermute | solution.py:350
  0.5 15.2 %collective-permute-start.1 = (bf16[128,1024]{1,0:T(8,128)(2,1)}, bf16[128,1024]{1,0:T(8,128)(2,1)S(1)}, u32[]{:S(2)}, u32[]{:S(2)}) collective-permute-start(bf16[128,1024]{1,0:T(8,128)(2,1)} %o.1), channel_id=1, source_target_pairs={{0,4},{1,3},{2,6},{3,1},{4,0},{5,7},{6,2},{7,5},{8,12},{9,11},{10,... | collective-permute-start | bytes 786440 | tf_op jit(solution)/shard_map/ppermute | solution.py:354
  3.0 12.7 %collective-permute-start.3 = (bf16[128,1024]{1,0:T(8,128)(2,1)}, bf16[128,1024]{1,0:T(8,128)(2,1)S(1)}, u32[]{:S(2)}, u32[]{:S(2)}) collective-permute-start(bf16[128,1024]{1,0:T(8,128)(2,1)} %o.1), channel_id=1, source_target_pairs={{0,6},{1,7},{2,4},{3,5},{4,2},{5,3},{6,0},{7,1},{8,14},{9,15},{10,... | collective-permute-start | bytes 786440 | tf_op jit(solution)/shard_map/ppermute | solution.py:350
  4.4 11.4 %collective-permute-start.2 = (bf16[128,1024]{1,0:T(8,128)(2,1)}, bf16[128,1024]{1,0:T(8,128)(2,1)S(1)}, u32[]{:S(2)}, u32[]{:S(2)}) collective-permute-start(bf16[128,1024]{1,0:T(8,128)(2,1)} %o.1), channel_id=1, source_target_pairs={{0,2},{1,5},{2,0},{3,7},{4,6},{5,1},{6,4},{7,3},{8,10},{9,13},{10,... | collective-permute-start | bytes 786440 | tf_op jit(solution)/shard_map/ppermute | solution.py:354
  15.8 2.4 %collective-permute-start.4 = (bf16[3,128,1024]{2,1,0:T(8,128)(2,1)S(1)}, bf16[3,128,1024]{2,1,0:T(8,128)(2,1)S(1)}, u32[]{:S(2)}, u32[]{:S(2)}) collective-permute-start(bf16[3,128,1024]{2,1,0:T(8,128)(2,1)S(1)} %pack_kernel.1.packed.own), channel_id=1, source_target_pairs={{0,1},{1,0},{2,3},{3,2},{4,5},{5,4},{6,7},{7,6},{8,9},{9,8},{10,11... | collective-permute-start | bytes 2359304 | tf_op jit(solution)/shard_map/ppermute | solution.py:350
  18.3 7.9 %copy-start = (f32[1024]{0:T(1024)S(1)}, f32[1024]{0:T(1024)}, u32[]{:S(2)}) copy-start(f32[1024]{0:T(1024)} %param.10) | copy-start | bytes 12292
  21.6 8.2 %collective-permute-start.5 = (f32[16,8,128]{2,1,0:T(8,128)S(1)}, f32[16,8,128]{2,1,0:T(8,128)S(1)}, u32[]{:S(2)}, u32[]{:S(2)}) collective-permute-start(f32[16,8,128]{2,1,0:T(8,128)S(1)} %get-tuple-element.42), channel_id=1, source_target_pairs={{0,8},{8,16},{16,24},{24,0},{1,9},{9,17},{17,25},{25,1},{2,10},{10... | collective-permute-start | bytes 196616 | tf_op jit(solution)/shard_map/ppermute | solution.py:419
  23.6 6.2 %collective-permute-start.6 = (bf16[16,8,128]{2,1,0:T(8,128)(2,1)S(1)}, bf16[16,8,128]{2,1,0:T(8,128)(2,1)S(1)}, u32[]{:S(2)}, u32[]{:S(2)}) collective-permute-start(bf16[16,8,128]{2,1,0:T(8,128)(2,1)S(1)} %convert_element_type.3), channel_id=1, source_target_pairs={{0,16},{8,24},{16,0},{24,8},{1,17},{9,25},{17,1},{25,9},{2,18},{10... | collective-permute-start | bytes 98312 | tf_op jit(solution)/shard_map/ppermute | solution.py:419

commit v6 on v5

--- a/solution.py
+++ b/solution.py
@@ -9,6 +9,7 @@
 
 SUB = 8
 LANE = 128
+PIECE = 32
 IN_VMEM = pl.BlockSpec(memory_space=pltpu.VMEM)
 IN_HBM = pl.BlockSpec(memory_space=pltpu.HBM)
 DRIVEN = (1, 2)
@@ -221,15 +222,15 @@
     modes = lam3.shape[0]
 
     def body(step, state):
-        first = pl.multiple_of(step * SUB, SUB)
-        counts = rowmask[0, pl.ds(first, SUB), :]
-        for j in range(SUB):
+        first = pl.multiple_of(step * 32, 32)
+        counts = rowmask[0, pl.ds(first, 32), :]
+        for j in range(32):
             drive = d3[first + j] * counts[j : j + 1, :]
             state = [lam3[n] * state[n] + drive for n in range(modes)]
         return state
 
     zeros = [jnp.zeros((SUB, LANE), jnp.float32) for _ in range(modes)]
-    state = lax.fori_loop(0, rows // SUB, body, zeros)
+    state = lax.fori_loop(0, rows // 32, body, zeros)
     for n in range(modes):
         e3[n] = state[n]
     for i in range(3):
@@ -273,9 +274,9 @@
     wait = run_copies(weight_copies(wt, GATE, own_masks()[:1] + other_masks()[1:], depth, wbuf, sem), 8)
 
     def body(step, state):
-        first = pl.multiple_of(step * SUB, SUB)
-        keeps = rowmask[1, pl.ds(first, SUB), :]
-        for j in range(SUB):
+        first = pl.multiple_of(step * 32, 32)
+        keeps = rowmask[1, pl.ds(first, 32), :]
+        for j in range(32):
             drive = d3[first + j]
             state = [lam3[n] * (state[n] * keeps[j : j + 1, :]) + drive for n in range(modes)]
             terms = [mix3[n] * state[n] for n in range(modes)]
@@ -285,7 +286,7 @@
         return state
 
     zeros = [jnp.zeros((SUB, LANE), jnp.float32) for _ in range(modes)]
-    lax.fori_loop(0, rows // SUB, body, zeros)
+    lax.fori_loop(0, rows // 32, body, zeros)
     total = sum_in[...] + project((b, d, ao), gate_far, 0)
     for i, block in enumerate((a, bo, do)):
         wait(i)
@@ -295,7 +296,7 @@
 
 def last_kernel(*refs, count):
     arrived = refs[:count]
-    outer, f3, scale, lam3, mix3, rowmask, valid, out = refs[count:]
+    outer, f3, scale, lam3, mix3, rowmask, valid, out, buf, sem = refs[count:]
     rows = outer.shape[0]
     modes = lam3.shape[0]
     @pl.when(lax.axis_index("ctx") > 0)
@@ -314,9 +315,9 @@
             state.append(mix3[n] * total)
 
         def body(step, state):
-            first = pl.multiple_of(step * SUB, SUB)
-            reached = rowmask[2, pl.ds(first, SUB), :]
-            for j in range(SUB):
+            first = pl.multiple_of(step * 32, 32)
+            reached = rowmask[2, pl.ds(first, 32), :]
+            for j in range(32):
                 t = first + j
                 state = [lam3[n] * state[n] for n in range(modes)]
                 terms = list(state)
@@ -325,11 +326,18 @@
                 f3[t] = f3[t] + terms[0] * reached[j : j + 1, :]
             return state
 
-        lax.fori_loop(0, rows // SUB, body, state)
-
-    for g in range(SUB):
-        cols = slice(g * LANE, (g + 1) * LANE)
-        out[:, cols] = (outer[:, cols] * scale[...] * f3[:, g, :]).astype(out.dtype)
+        lax.fori_loop(0, rows // 32, body, state)
+
+    copies = []
+    for r in range(0, rows, PIECE):
+        piece = slice(r, r + PIECE)
+        for g in range(SUB):
+            cols = slice(g * LANE, (g + 1) * LANE)
+            buf[piece, cols] = (outer[piece, cols] * scale[piece] * f3[piece, g, :]).astype(buf.dtype)
+        copies.append(pltpu.make_async_copy(buf.at[piece], out.at[piece], sem.at[r // PIECE]))
+        copies[-1].start()
+    for c in copies:
+        c.wait()
 
 
 def params(mib):
@@ -432,8 +440,9 @@
     return pl.pallas_call(
         functools.partial(last_kernel, count=reach),
         in_specs=[IN_VMEM] * (reach + 7),
-        out_specs=IN_VMEM,
+        out_specs=IN_HBM,
         out_shape=jax.ShapeDtypeStruct((rows, local), b16),
+        scratch_shapes=[chunk, dma((rows // PIECE,))],
         compiler_params=params(8),
         name="last",
     )(*arrived, outer, f3, scale, lam3, mix3, rowmask, valid)

time: 31 us -> 30.8 us (level)
  no operation moved by 1% of the time
where the time goes in v6:
time: 30.8 us; the launch traced here: 30.6 us
  Pallas kernels  21.1 us (69%)
  starting transfers between devices  9.29 us (30%)
    pallas_call x5, Pallas kernels, call(): pl.pallas_call(kernel, in_specs=[spec for spec, _ in ins], out_specs=[IN_...  20.1 us
    ppermute x2, starting transfers between devices, fitted(): lax.ppermute(e3 if k == 1 else e3.astype(b16), 'ctx', [(i, (i + k) % ring...  4.61 us
    ppermute x2, starting transfers between devices, split(): lax.ppermute(block, 'ch', [(i, i ^ masks[i & 1]) for i in range(size)])  2.62 us
    ppermute x3, starting transfers between devices, swap(): return lax.ppermute(block, 'ch', [(i, i ^ mask) for i in range(size)])  2.07 us
    pallas_call x1, Pallas kernels, fitted(): pl.pallas_call(functools.partial(last_kernel, count=reach), in_specs=[IN_...  1.02 us
  transfers between devices with their start and end apart: 7, of which 1 were waited for; matrix products, arithmetic and copies ran while one was open for 0% of the time, Pallas kernels for 55%

profile of v6, /device:TPU:0, one launch (start us, length us, event | category | flops | bytes accessed | tf_op | source)
XLA Modules:
  0.0 30.6 jit_solution(883251294863019087)
XLA Ops:
  0.0 0.5 %collective-permute-start = (bf16[128,1024]{1,0:T(8,128)(2,1)}, bf16[128,1024]{1,0:T(8,128)(2,1)S(1)}, u32[]{:S(2)}, u32[]{:S(2)}) collective-permute-start(bf16[128,1024]{1,0:T(8,128)(2,1)} %o.1), channel_id=1, source_target_pairs={{0,1},{1,0},{2,3},{3,2},{4,5},{5,4},{6,7},{7,6},{8,9},{9,8},{10,11... | collective-permute-start | bytes 786440 | tf_op jit(solution)/shard_map/ppermute | solution.py:358
  0.5 2.5 %collective-permute-start.1 = (bf16[128,1024]{1,0:T(8,128)(2,1)}, bf16[128,1024]{1,0:T(8,128)(2,1)S(1)}, u32[]{:S(2)}, u32[]{:S(2)}) collective-permute-start(bf16[128,1024]{1,0:T(8,128)(2,1)} %o.1), channel_id=1, source_target_pairs={{0,4},{1,3},{2,6},{3,1},{4,0},{5,7},{6,2},{7,5},{8,12},{9,11},{10,... | collective-permute-start | bytes 786440 | tf_op jit(solution)/shard_map/ppermute | solution.py:362
  3.0 1.4 %collective-permute-start.3 = (bf16[128,1024]{1,0:T(8,128)(2,1)}, bf16[128,1024]{1,0:T(8,128)(2,1)S(1)}, u32[]{:S(2)}, u32[]{:S(2)}) collective-permute-start(bf16[128,1024]{1,0:T(8,128)(2,1)} %o.1), channel_id=1, source_target_pairs={{0,6},{1,7},{2,4},{3,5},{4,2},{5,3},{6,0},{7,1},{8,14},{9,15},{10,... | collective-permute-start | bytes 786440 | tf_op jit(solution)/shard_map/ppermute | solution.py:358
  4.4 0.1 collective-permute-start.2
  4.5 0.0 collective-permute-done.s
  4.5 11.1 %first_kernel.1 = (f32[2,128,1024]{2,1,0:T(8,128)S(1)}, f32[128,1024]{1,0:T(8,128)S(1)}, f32[128,128]{1,0:T(8,128)S(1)}, f32[16,8,128]{2,1,0:T(8,128)S(1)}, f32[...) custom-call(bf16[128,1024]{1,0:T(8,128)(2,1)} %o.1, ...), custom_call_target="tpu_custom_call" | custom-call | flops 1073741824 | tf_op jit(solution)/shard_map/first_kernel/pallas_call | solution.py:365
  15.7 0.0 collective-permute-done.1.a
  15.7 0.0 collective-permute-done.3.d
  15.7 0.1 collective-permute-done.2.b
  15.8 0.1 pack_kernel.1.packed.own
  15.8 0.2 collective-permute-start.4
  16.0 2.2 %near_kernel.1 = (f32[2,128,1024]{2,1,0:T(8,128)S(1)}, f32[128,128]{1,0:T(8,128)S(1)}, bf16[2,1024,1024]{2,1,0:T(8,128)(2,1)S(1)}) custom-call(bf16[3,128,1024]{2,1,0:T(8,128)(2,1)S(1)} %pack_kernel.1.packed.own, bf16[2,3072,1024]{2,1,0:T(8,128)(2,1)S(1)} %get-tuple-element.34.weights, bf16[3,8192,1024]{2,1,0:T(8,128)(2,1)} %bitcast.6, ...), custom_call_target="tpu_custom_call" | custom-call | flops 1610612736 | tf_op jit(solution)/shard_map/near_kernel/pallas_call | solution.py:365
  18.3 0.0 collective-permute-done.4.packed.others
  18.3 0.0 copy-start
  18.3 3.2 %far_kernel.1 = (f32[128,128]{1,0:T(8,128)S(1)}, f32[128,8,128]{2,1,0:T(8,128)S(1)}, f32[16,8,128]{2,1,0:T(8,128)S(1)}, bf16[1,3072,1024]{2,1,0:T(8,128)(2,1)S(1)}) custom-call(bf16[2,2048,1024]{2,1,0:T(8,128)(2,1)S(1)} %get-tuple-element.28.weights, bf16[3,128,1024]{2,1,0:T(8,128)(2,1)S(1)} %collective-permute-done.4.packed.others, ...), custom_call_target="tpu_custom_call" | custom-call | flops 1610612736 | tf_op jit(solution)/shard_map/far_kernel/pallas_call | solution.py:365
  21.5 2.0 %collective-permute-start.5 = (f32[16,8,128]{2,1,0:T(8,128)S(1)}, f32[16,8,128]{2,1,0:T(8,128)S(1)}, u32[]{:S(2)}, u32[]{:S(2)}) collective-permute-start(f32[16,8,128]{2,1,0:T(8,128)S(1)} %get-tuple-element.42), channel_id=1, source_target_pairs={{0,8},{8,16},{16,24},{24,0},{1,9},{9,17},{17,25},{25,1},{2,10},{10... | collective-permute-start | bytes 196616 | tf_op jit(solution)/shard_map/ppermute | solution.py:427
  23.5 2.6 %collective-permute-start.6 = (bf16[16,8,128]{2,1,0:T(8,128)(2,1)S(1)}, bf16[16,8,128]{2,1,0:T(8,128)(2,1)S(1)}, u32[]{:S(2)}, u32[]{:S(2)}) collective-permute-start(bf16[16,8,128]{2,1,0:T(8,128)(2,1)S(1)} %convert_element_type.3), channel_id=1, source_target_pairs={{0,16},{8,24},{16,0},{24,8},{1,17},{9,25},{17,1},{25,9},{2,18},{10... | collective-permute-start | bytes 98312 | tf_op jit(solution)/shard_map/ppermute | solution.py:427
  26.1 0.0 copy-done
  26.1 3.5 %outer_kernel.1 = (f32[128,1024]{1,0:T(8,128)S(1)}, f32[128,8,128]{2,1,0:T(8,128)S(1)}) custom-call(bf16[3,128,1024]{2,1,0:T(8,128)(2,1)S(1)} %pack_kernel.1.packed.own, bf16[3,128,1024]{2,1,0:T(8,128)(2,1)S(1)} %collective-permute-done.4.packed.others, bf16[3,8192,1024]{2,1,0:T(8,128)(2,1)} %bitcast.8, f32[128,1024]{1,0:T(8,128)S(1)} %get-tuple-element.43.sum_in, ...), custom_call_target="tpu_custom_call" | custom-call | flops 1610612736 | tf_op jit(solution)/shard_map/outer_kernel/pallas_call | solution.py:365
  29.6 0.0 collective-permute-done.6.refs_1_
  29.6 0.0 collective-permute-done.5.refs_0_
  29.6 1.0 %last.1 = bf16[128,1024]{1,0:T(8,128)(2,1)} custom-call(f32[16,8,128]{2,1,0:T(8,128)S(1)} %collective-permute-done.5.refs_0_, bf16[16,8,128]{2,1,0:T(8,128)(2,1)S(1)} %collective-permute-done.6.refs_1_, f32[128,1024]{1,0:T(8,128)S(1)} %get-tuple-element.47.refs_2_, f32[128,8,128]{2,1,0:T(8,128)S(1)} %get-tuple-element.48.refs_3_, ...), custom_call_target="tpu_custom_call" | custom-call | tf_op jit(solution)/shard_map/last/pallas_call | solution.py:440
  (1 shorter events, 0.0 us)
Async XLA Ops:
  0.0 4.5 %collective-permute-start = (bf16[128,1024]{1,0:T(8,128)(2,1)}, bf16[128,1024]{1,0:T(8,128)(2,1)S(1)}, u32[]{:S(2)}, u32[]{:S(2)}) collective-permute-start(bf16[128,1024]{1,0:T(8,128)(2,1)} %o.1), channel_id=1, source_target_pairs={{0,1},{1,0},{2,3},{3,2},{4,5},{5,4},{6,7},{7,6},{8,9},{9,8},{10,11... | collective-permute-start | bytes 786440 | tf_op jit(solution)/shard_map/ppermute | solution.py:358
  0.5 15.2 %collective-permute-start.1 = (bf16[128,1024]{1,0:T(8,128)(2,1)}, bf16[128,1024]{1,0:T(8,128)(2,1)S(1)}, u32[]{:S(2)}, u32[]{:S(2)}) collective-permute-start(bf16[128,1024]{1,0:T(8,128)(2,1)} %o.1), channel_id=1, source_target_pairs={{0,4},{1,3},{2,6},{3,1},{4,0},{5,7},{6,2},{7,5},{8,12},{9,11},{10,... | collective-permute-start | bytes 786440 | tf_op jit(solution)/shard_map/ppermute | solution.py:362
  3.0 12.7 %collective-permute-start.3 = (bf16[128,1024]{1,0:T(8,128)(2,1)}, bf16[128,1024]{1,0:T(8,128)(2,1)S(1)}, u32[]{:S(2)}, u32[]{:S(2)}) collective-permute-start(bf16[128,1024]{1,0:T(8,128)(2,1)} %o.1), channel_id=1, source_target_pairs={{0,6},{1,7},{2,4},{3,5},{4,2},{5,3},{6,0},{7,1},{8,14},{9,15},{10,... | collective-permute-start | bytes 786440 | tf_op jit(solution)/shard_map/ppermute | solution.py:358
  4.4 11.4 %collective-permute-start.2 = (bf16[128,1024]{1,0:T(8,128)(2,1)}, bf16[128,1024]{1,0:T(8,128)(2,1)S(1)}, u32[]{:S(2)}, u32[]{:S(2)}) collective-permute-start(bf16[128,1024]{1,0:T(8,128)(2,1)} %o.1), channel_id=1, source_target_pairs={{0,2},{1,5},{2,0},{3,7},{4,6},{5,1},{6,4},{7,3},{8,10},{9,13},{10,... | collective-permute-start | bytes 786440 | tf_op jit(solution)/shard_map/ppermute | solution.py:362
  15.8 2.4 %collective-permute-start.4 = (bf16[3,128,1024]{2,1,0:T(8,128)(2,1)S(1)}, bf16[3,128,1024]{2,1,0:T(8,128)(2,1)S(1)}, u32[]{:S(2)}, u32[]{:S(2)}) collective-permute-start(bf16[3,128,1024]{2,1,0:T(8,128)(2,1)S(1)} %pack_kernel.1.packed.own), channel_id=1, source_target_pairs={{0,1},{1,0},{2,3},{3,2},{4,5},{5,4},{6,7},{7,6},{8,9},{9,8},{10,11... | collective-permute-start | bytes 2359304 | tf_op jit(solution)/shard_map/ppermute | solution.py:358
  18.3 7.8 %copy-start = (f32[1024]{0:T(1024)S(1)}, f32[1024]{0:T(1024)}, u32[]{:S(2)}) copy-start(f32[1024]{0:T(1024)} %param.10) | copy-start | bytes 12292
  21.5 8.1 %collective-permute-start.5 = (f32[16,8,128]{2,1,0:T(8,128)S(1)}, f32[16,8,128]{2,1,0:T(8,128)S(1)}, u32[]{:S(2)}, u32[]{:S(2)}) collective-permute-start(f32[16,8,128]{2,1,0:T(8,128)S(1)} %get-tuple-element.42), channel_id=1, source_target_pairs={{0,8},{8,16},{16,24},{24,0},{1,9},{9,17},{17,25},{25,1},{2,10},{10... | collective-permute-start | bytes 196616 | tf_op jit(solution)/shard_map/ppermute | solution.py:427
  23.5 6.1 %collective-permute-start.6 = (bf16[16,8,128]{2,1,0:T(8,128)(2,1)S(1)}, bf16[16,8,128]{2,1,0:T(8,128)(2,1)S(1)}, u32[]{:S(2)}, u32[]{:S(2)}) collective-permute-start(bf16[16,8,128]{2,1,0:T(8,128)(2,1)S(1)} %convert_element_type.3), channel_id=1, source_target_pairs={{0,16},{8,24},{16,0},{24,8},{1,17},{9,25},{17,1},{25,9},{2,18},{10... | collective-permute-start | bytes 98312 | tf_op jit(solution)/shard_map/ppermute | solution.py:427

commit v7 on v6

--- a/solution.py
+++ b/solution.py
@@ -140,7 +140,7 @@
 
 
 def first_kernel(
-    o, s, wt, rate, res, lengths, acc, outer, sq, lam3, mix3, near, far, rowmask, valid, held, wbuf, gbuf, rates, ress, docs, sem, small
+    o, s, wt, rate, res, lengths, acc, outer, sq, lam3, mix3, near, far, rowmask, valid, begins, held, wbuf, gbuf, rates, ress, docs, sem, small
 ):
     rows, depth = s.shape
     own = [
@@ -172,7 +172,7 @@
 
     by_groups(lam, put_lam)
     by_groups(mix, put_mix)
-    mark_rows(docs, rows, rowmask, valid)
+    mark_rows(docs, rows, rowmask, valid, begins)
     for k in range(2):
         wait(2 * k)
         wait(2 * k + 1)
@@ -237,7 +237,7 @@
         wait(i)
 
 
-def mark_rows(docs, rows, rowmask, valid):
+def mark_rows(docs, rows, rowmask, valid, begins):
     me = lax.axis_index("ctx")
     at = -me * rows
     first, last, starts = rows, -1, []
@@ -247,6 +247,12 @@
         last = jnp.where(jnp.logical_and(inside, at > last), at, last)
         starts.append(at)
         at = at + docs[i]
+    span = rows // begins.shape[0]
+    for g in range(begins.shape[0]):
+        begins[g] = jnp.int32(0)
+        for at in starts:
+            inside = jnp.logical_and(at >= g * span, at < (g + 1) * span)
+            begins[g] = jnp.where(inside, 1, begins[g])
     token = lax.broadcasted_iota(jnp.int32, rowmask.shape[1:], 0)
     rowmask[0] = jnp.where(token >= last, 1.0, 0.0)
     keep = jnp.ones(rowmask.shape[1:], jnp.float32)
@@ -265,7 +271,7 @@
 
 
 def outer_kernel(
-    own, others, wt, sum_in, gate_far, d3, lam3, mix3, skip, rowmask, outer, f3, wbuf, sem
+    own, others, wt, sum_in, gate_far, d3, lam3, mix3, skip, rowmask, begins, outer, f3, wbuf, sem
 ):
     _, rows, depth = own.shape
     a, b, d = [own.at[i] for i in range(3)]
@@ -273,19 +279,26 @@
     modes = lam3.shape[0]
     wait = run_copies(weight_copies(wt, GATE, own_masks()[:1] + other_masks()[1:], depth, wbuf, sem), 8)
 
-    def body(step, state):
+    def tokens(step, state, resets):
         first = pl.multiple_of(step * 32, 32)
         keeps = rowmask[1, pl.ds(first, 32), :]
         for j in range(32):
             drive = d3[first + j]
-            state = [lam3[n] * (state[n] * keeps[j : j + 1, :]) + drive for n in range(modes)]
+            if resets:
+                state = [s * keeps[j : j + 1, :] for s in state]
+            state = [lam3[n] * state[n] + drive for n in range(modes)]
             terms = [mix3[n] * state[n] for n in range(modes)]
             while len(terms) > 1:
                 terms = [p + q for p, q in zip(terms[::2], terms[1::2])]
             f3[first + j] = terms[0] + skip[...] * drive
-        return state
-
-    zeros = [jnp.zeros((SUB, LANE), jnp.float32) for _ in range(modes)]
+        return tuple(state)
+
+    def body(step, state):
+        return lax.cond(
+            begins[step] > 0, lambda s: tokens(step, s, True), lambda s: tokens(step, s, False), state
+        )
+
+    zeros = tuple(jnp.zeros((SUB, LANE), jnp.float32) for _ in range(modes))
     lax.fori_loop(0, rows // 32, body, zeros)
     total = sum_in[...] + project((b, d, ao), gate_far, 0)
     for i, block in enumerate((a, bo, do)):
@@ -365,7 +378,7 @@
         return pl.pallas_call(
             kernel,
             in_specs=[spec for spec, _ in ins],
-            out_specs=[IN_VMEM] * len(outs),
+            out_specs=[pl.BlockSpec(memory_space=o.memory_space) for o in outs],
             out_shape=outs,
             scratch_shapes=scratch,
             compiler_params=params(mib),
@@ -394,11 +407,12 @@
 
     s = swap(stream, 1)
     a, b, d = split(stream, True), split(stream, False), swap(stream, 6)
-    acc, outer, sq, lam3, mix3, near, far, rowmask, valid = call(
+    acc, outer, sq, lam3, mix3, near, far, rowmask, valid, begins = call(
         first_kernel,
         there(stream) + here(s) + there(wt, rate, res, doc_lengths),
         [planes, product, squares, poles, poles, weights(2, 3), weights(2, 2)]
-        + [pltpu.VMEM((3, rows, LANE), f32), pltpu.VMEM((reach, SUB, LANE), f32)],
+        + [pltpu.VMEM((3, rows, LANE), f32), pltpu.VMEM((reach, SUB, LANE), f32)]
+        + [pltpu.SMEM((rows // 32,), jnp.int32)],
         [chunk, weights(2, 2), weights(1, 2), vector, vector, pltpu.SMEM(doc_lengths.shape, jnp.int32), dma((16,)), dma((4,))],
         4,
         16,
@@ -431,7 +445,8 @@
         outer_kernel,
         here(own, others)
         + there(wt)
-        + here(outer, gate_far, d3, lam3, mix3, skip_gain.reshape(SUB, LANE), rowmask),
+        + here(outer, gate_far, d3, lam3, mix3, skip_gain.reshape(SUB, LANE), rowmask)
+        + [(pl.BlockSpec(memory_space=pltpu.SMEM), begins)],
         [product, tokens],
         [weights(1, 3), dma((3,))],
         6,

time: 30.8 us -> 30.7 us (level)
  no operation moved by 1% of the time
where the time goes in v7:
time: 30.7 us; the launch traced here: 30.6 us
  Pallas kernels  21 us (68%)
  starting transfers between devices  9.29 us (30%)
    pallas_call x5, Pallas kernels, call(): pl.pallas_call(kernel, in_specs=[spec for spec, _ in ins], out_specs=[pl....  20 us
    ppermute x2, starting transfers between devices, fitted(): lax.ppermute(e3 if k == 1 else e3.astype(b16), 'ctx', [(i, (i + k) % ring...  4.61 us
    ppermute x2, starting transfers between devices, split(): lax.ppermute(block, 'ch', [(i, i ^ masks[i & 1]) for i in range(size)])  2.62 us
    ppermute x3, starting transfers between devices, swap(): return lax.ppermute(block, 'ch', [(i, i ^ mask) for i in range(size)])  2.07 us
    pallas_call x1, Pallas kernels, fitted(): pl.pallas_call(functools.partial(last_kernel, count=reach), in_specs=[IN_...  1.01 us
  transfers between devices with their start and end apart: 7, of which 1 were waited for; matrix products, arithmetic and copies ran while one was open for 0% of the time, Pallas kernels for 55%

profile of v7, /device:TPU:0, one launch (start us, length us, event | category | flops | bytes accessed | tf_op | source)
XLA Modules:
  0.0 30.6 jit_solution(12935647923447910091)
XLA Ops:
  0.0 0.5 %collective-permute-start = (bf16[128,1024]{1,0:T(8,128)(2,1)}, bf16[128,1024]{1,0:T(8,128)(2,1)S(1)}, u32[]{:S(2)}, u32[]{:S(2)}) collective-permute-start(bf16[128,1024]{1,0:T(8,128)(2,1)} %o.1), channel_id=1, source_target_pairs={{0,1},{1,0},{2,3},{3,2},{4,5},{5,4},{6,7},{7,6},{8,9},{9,8},{10,11... | collective-permute-start | bytes 786440 | tf_op jit(solution)/shard_map/ppermute | solution.py:371
  0.5 2.5 %collective-permute-start.1 = (bf16[128,1024]{1,0:T(8,128)(2,1)}, bf16[128,1024]{1,0:T(8,128)(2,1)S(1)}, u32[]{:S(2)}, u32[]{:S(2)}) collective-permute-start(bf16[128,1024]{1,0:T(8,128)(2,1)} %o.1), channel_id=1, source_target_pairs={{0,4},{1,3},{2,6},{3,1},{4,0},{5,7},{6,2},{7,5},{8,12},{9,11},{10,... | collective-permute-start | bytes 786440 | tf_op jit(solution)/shard_map/ppermute | solution.py:375
  3.0 1.4 %collective-permute-start.3 = (bf16[128,1024]{1,0:T(8,128)(2,1)}, bf16[128,1024]{1,0:T(8,128)(2,1)S(1)}, u32[]{:S(2)}, u32[]{:S(2)}) collective-permute-start(bf16[128,1024]{1,0:T(8,128)(2,1)} %o.1), channel_id=1, source_target_pairs={{0,6},{1,7},{2,4},{3,5},{4,2},{5,3},{6,0},{7,1},{8,14},{9,15},{10,... | collective-permute-start | bytes 786440 | tf_op jit(solution)/shard_map/ppermute | solution.py:371
  4.4 0.1 collective-permute-start.2
  4.5 0.0 collective-permute-done.s
  4.5 11.1 %first_kernel.1 = (f32[2,128,1024]{2,1,0:T(8,128)S(1)}, f32[128,1024]{1,0:T(8,128)S(1)}, f32[128,128]{1,0:T(8,128)S(1)}, f32[16,8,128]{2,1,0:T(8,128)S(1)}, f32[...) custom-call(bf16[128,1024]{1,0:T(8,128)(2,1)} %o.1, ...), custom_call_target="tpu_custom_call" | custom-call | flops 1073741824 | tf_op jit(solution)/shard_map/first_kernel/pallas_call | solution.py:378
  15.7 0.0 collective-permute-done.1.a
  15.7 0.0 collective-permute-done.3.d
  15.7 0.1 collective-permute-done.2.b
  15.8 0.1 pack_kernel.1.packed.own
  15.8 0.2 collective-permute-start.4
  16.0 2.2 %near_kernel.1 = (f32[2,128,1024]{2,1,0:T(8,128)S(1)}, f32[128,128]{1,0:T(8,128)S(1)}, bf16[2,1024,1024]{2,1,0:T(8,128)(2,1)S(1)}) custom-call(bf16[3,128,1024]{2,1,0:T(8,128)(2,1)S(1)} %pack_kernel.1.packed.own, bf16[2,3072,1024]{2,1,0:T(8,128)(2,1)S(1)} %get-tuple-element.35.weights, bf16[3,8192,1024]{2,1,0:T(8,128)(2,1)} %bitcast.6, ...), custom_call_target="tpu_custom_call" | custom-call | flops 1610612736 | tf_op jit(solution)/shard_map/near_kernel/pallas_call | solution.py:378
  18.3 0.0 collective-permute-done.4.packed.others
  18.3 0.0 copy-start
  18.3 3.2 %far_kernel.1 = (f32[128,128]{1,0:T(8,128)S(1)}, f32[128,8,128]{2,1,0:T(8,128)S(1)}, f32[16,8,128]{2,1,0:T(8,128)S(1)}, bf16[1,3072,1024]{2,1,0:T(8,128)(2,1)S(1)}) custom-call(bf16[2,2048,1024]{2,1,0:T(8,128)(2,1)S(1)} %get-tuple-element.29.weights, bf16[3,128,1024]{2,1,0:T(8,128)(2,1)S(1)} %collective-permute-done.4.packed.others, ...), custom_call_target="tpu_custom_call" | custom-call | flops 1610612736 | tf_op jit(solution)/shard_map/far_kernel/pallas_call | solution.py:378
  21.5 2.0 %collective-permute-start.5 = (f32[16,8,128]{2,1,0:T(8,128)S(1)}, f32[16,8,128]{2,1,0:T(8,128)S(1)}, u32[]{:S(2)}, u32[]{:S(2)}) collective-permute-start(f32[16,8,128]{2,1,0:T(8,128)S(1)} %get-tuple-element.43), channel_id=1, source_target_pairs={{0,8},{8,16},{16,24},{24,0},{1,9},{9,17},{17,25},{25,1},{2,10},{10... | collective-permute-start | bytes 196616 | tf_op jit(solution)/shard_map/ppermute | solution.py:441
  23.5 2.6 %collective-permute-start.6 = (bf16[16,8,128]{2,1,0:T(8,128)(2,1)S(1)}, bf16[16,8,128]{2,1,0:T(8,128)(2,1)S(1)}, u32[]{:S(2)}, u32[]{:S(2)}) collective-permute-start(bf16[16,8,128]{2,1,0:T(8,128)(2,1)S(1)} %convert_element_type.3), channel_id=1, source_target_pairs={{0,16},{8,24},{16,0},{24,8},{1,17},{9,25},{17,1},{25,9},{2,18},{10... | collective-permute-start | bytes 98312 | tf_op jit(solution)/shard_map/ppermute | solution.py:441
  26.1 0.0 copy-done
  26.1 3.4 %outer_kernel.1 = (f32[128,1024]{1,0:T(8,128)S(1)}, f32[128,8,128]{2,1,0:T(8,128)S(1)}) custom-call(bf16[3,128,1024]{2,1,0:T(8,128)(2,1)S(1)} %pack_kernel.1.packed.own, bf16[3,128,1024]{2,1,0:T(8,128)(2,1)S(1)} %collective-permute-done.4.packed.others, bf16[3,8192,1024]{2,1,0:T(8,128)(2,1)} %bitcast.8, f32[128,1024]{1,0:T(8,128)S(1)} %get-tuple-element.44.sum_in, ...), custom_call_target="tpu_custom_call" | custom-call | flops 1610612736 | tf_op jit(solution)/shard_map/outer_kernel/pallas_call | solution.py:378
  29.5 0.0 collective-permute-done.6.refs_1_
  29.6 0.0 collective-permute-done.5.refs_0_
  29.6 1.0 %last.1 = bf16[128,1024]{1,0:T(8,128)(2,1)} custom-call(f32[16,8,128]{2,1,0:T(8,128)S(1)} %collective-permute-done.5.refs_0_, bf16[16,8,128]{2,1,0:T(8,128)(2,1)S(1)} %collective-permute-done.6.refs_1_, f32[128,1024]{1,0:T(8,128)S(1)} %get-tuple-element.49.refs_2_, f32[128,8,128]{2,1,0:T(8,128)S(1)} %get-tuple-element.50.refs_3_, ...), custom_call_target="tpu_custom_call" | custom-call | tf_op jit(solution)/shard_map/last/pallas_call | solution.py:455
  (1 shorter events, 0.0 us)
Async XLA Ops:
  0.0 4.5 %collective-permute-start = (bf16[128,1024]{1,0:T(8,128)(2,1)}, bf16[128,1024]{1,0:T(8,128)(2,1)S(1)}, u32[]{:S(2)}, u32[]{:S(2)}) collective-permute-start(bf16[128,1024]{1,0:T(8,128)(2,1)} %o.1), channel_id=1, source_target_pairs={{0,1},{1,0},{2,3},{3,2},{4,5},{5,4},{6,7},{7,6},{8,9},{9,8},{10,11... | collective-permute-start | bytes 786440 | tf_op jit(solution)/shard_map/ppermute | solution.py:371
  0.5 15.2 %collective-permute-start.1 = (bf16[128,1024]{1,0:T(8,128)(2,1)}, bf16[128,1024]{1,0:T(8,128)(2,1)S(1)}, u32[]{:S(2)}, u32[]{:S(2)}) collective-permute-start(bf16[128,1024]{1,0:T(8,128)(2,1)} %o.1), channel_id=1, source_target_pairs={{0,4},{1,3},{2,6},{3,1},{4,0},{5,7},{6,2},{7,5},{8,12},{9,11},{10,... | collective-permute-start | bytes 786440 | tf_op jit(solution)/shard_map/ppermute | solution.py:375
  3.0 12.7 %collective-permute-start.3 = (bf16[128,1024]{1,0:T(8,128)(2,1)}, bf16[128,1024]{1,0:T(8,128)(2,1)S(1)}, u32[]{:S(2)}, u32[]{:S(2)}) collective-permute-start(bf16[128,1024]{1,0:T(8,128)(2,1)} %o.1), channel_id=1, source_target_pairs={{0,6},{1,7},{2,4},{3,5},{4,2},{5,3},{6,0},{7,1},{8,14},{9,15},{10,... | collective-permute-start | bytes 786440 | tf_op jit(solution)/shard_map/ppermute | solution.py:371
  4.4 11.4 %collective-permute-start.2 = (bf16[128,1024]{1,0:T(8,128)(2,1)}, bf16[128,1024]{1,0:T(8,128)(2,1)S(1)}, u32[]{:S(2)}, u32[]{:S(2)}) collective-permute-start(bf16[128,1024]{1,0:T(8,128)(2,1)} %o.1), channel_id=1, source_target_pairs={{0,2},{1,5},{2,0},{3,7},{4,6},{5,1},{6,4},{7,3},{8,10},{9,13},{10,... | collective-permute-start | bytes 786440 | tf_op jit(solution)/shard_map/ppermute | solution.py:375
  15.8 2.4 %collective-permute-start.4 = (bf16[3,128,1024]{2,1,0:T(8,128)(2,1)S(1)}, bf16[3,128,1024]{2,1,0:T(8,128)(2,1)S(1)}, u32[]{:S(2)}, u32[]{:S(2)}) collective-permute-start(bf16[3,128,1024]{2,1,0:T(8,128)(2,1)S(1)} %pack_kernel.1.packed.own), channel_id=1, source_target_pairs={{0,1},{1,0},{2,3},{3,2},{4,5},{5,4},{6,7},{7,6},{8,9},{9,8},{10,11... | collective-permute-start | bytes 2359304 | tf_op jit(solution)/shard_map/ppermute | solution.py:371
  18.3 7.8 %copy-start = (f32[1024]{0:T(1024)S(1)}, f32[1024]{0:T(1024)}, u32[]{:S(2)}) copy-start(f32[1024]{0:T(1024)} %param.10) | copy-start | bytes 12292
  21.5 8.1 %collective-permute-start.5 = (f32[16,8,128]{2,1,0:T(8,128)S(1)}, f32[16,8,128]{2,1,0:T(8,128)S(1)}, u32[]{:S(2)}, u32[]{:S(2)}) collective-permute-start(f32[16,8,128]{2,1,0:T(8,128)S(1)} %get-tuple-element.43), channel_id=1, source_target_pairs={{0,8},{8,16},{16,24},{24,0},{1,9},{9,17},{17,25},{25,1},{2,10},{10... | collective-permute-start | bytes 196616 | tf_op jit(solution)/shard_map/ppermute | solution.py:441
  23.5 6.0 %collective-permute-start.6 = (bf16[16,8,128]{2,1,0:T(8,128)(2,1)S(1)}, bf16[16,8,128]{2,1,0:T(8,128)(2,1)S(1)}, u32[]{:S(2)}, u32[]{:S(2)}) collective-permute-start(bf16[16,8,128]{2,1,0:T(8,128)(2,1)S(1)} %convert_element_type.3), channel_id=1, source_target_pairs={{0,16},{8,24},{16,0},{24,8},{1,17},{9,25},{17,1},{25,9},{2,18},{10... | collective-permute-start | bytes 98312 | tf_op jit(solution)/shard_map/ppermute | solution.py:441
